TPU v7x, 512 devices: a whole 4x8x8 slice. The times are simulated.
512 devices in a mesh: frame: 32 (over z_hi, y), height: 16 (over x, z_lo, core).
Axes of the slice: x: 4, y: 8, z: 8 (z_hi: 4, z_lo: 2; z = z_hi * 2 + z_lo), core: 2. Of those that a mesh axis runs over, the one named last changes fastest.
Arguments:
- queries: bfloat16 [32, 32, 80, 256], P('frame', 'height'), may hold values from -100 to 100
- keys: bfloat16 [32, 32, 80, 256], P('frame', 'height'), may hold values from -6 to 6
- values: bfloat16 [32, 32, 80, 256], P('frame', 'height'), may hold values from -6 to 6
- d_out: bfloat16 [32, 32, 80, 256], P('frame', 'height'), may hold values from -6 to 6
- reach: int32 [32, 16, 2, 2], P('frame', 'height'), may hold values from 0 to 1
Outputs:
- attended: bfloat16 [32, 32, 80, 256], P('frame', 'height')
- grad_queries: bfloat16 [32, 32, 80, 256], P('frame', 'height')
- grad_keys: bfloat16 [32, 32, 80, 256], P('frame', 'height')
- grad_values: bfloat16 [32, 32, 80, 256], P('frame', 'height')
All inputs are finite; a program needn't handle non-finite values.
Results may differ from a plain program's by a relative error of at most 0.04.
Values may be sent and summed in bfloat16 or wider, within the bound.
No kernel may reach another device: no remote copies, remote signals or barrier semaphores. Data moves between devices by JAX's collectives and lax.ppermute only.
A program may use at most 64 MiB of HBM per device.

v0:
```python
import jax
import jax.numpy as jnp
from jax import lax
from jax.sharding import PartitionSpec as P

WT = 8


def extended_2(shard, sides, width):
    for axis, dim in sides:
        size, length = (lax.axis_size(axis), shard.shape[dim])
        up = [(i, (i + 1) % size) for i in range(size - 1)]
        down = [(j, i) for i, j in up]
        last = lax.slice_in_dim(shard, length - width, length, axis=dim)
        first = lax.slice_in_dim(shard, 0, width, axis=dim)
        before = lax.ppermute(last, axis, up)
        after = lax.ppermute(first, axis, down)
        shard = jnp.concatenate([before, shard, after], axis=dim)
    return shard


def from_behind(shard, axis, by):
    length = lax.axis_size(axis)
    pairs = [(i, i + by) for i in range(length) if 0 <= i + by < length]
    return lax.ppermute(shard, axis, pairs)


def as_sent(shard):

    def short(part):
        return part.astype(jnp.bfloat16) if part.dtype == jnp.float32 else part

    return jax.tree.map(short, shard)


def to_groups(block, row_count, group_count, group_width):
    depth = block.shape[-1]
    split = block.reshape(row_count, group_count, group_width, depth)
    return split.transpose(1, 0, 2, 3).reshape(group_count, row_count * group_width, depth)


def from_groups(block, row_count, group_count, group_width):
    depth = block.shape[-1]
    split = block.reshape(group_count, row_count, group_width, depth)
    return split.transpose(1, 0, 2, 3).reshape(row_count * group_count * group_width, depth)


def band(block):
    group_count = block.shape[1]
    widths = [(0, 0), (1, 1)] + [(0, 0)] * (block.ndim - 2)
    padded = jnp.pad(block, widths)
    parts = jnp.stack([padded[:, shift_by : shift_by + group_count] for shift_by in range(3)])
    order = (2, 0, 1) + tuple(range(3, parts.ndim))
    return parts.transpose(order).reshape((group_count, -1) + block.shape[3:])


def band_mask(rows_ok, group_count, group_width):
    group_ids = (
        jnp.arange(group_count, dtype=jnp.int32)[:, None]
        + jnp.arange(3, dtype=jnp.int32)[None, :]
        - 1
    )
    valid = (group_ids >= 0) & (group_ids < group_count)
    full = valid[:, :, None, None] & rows_ok[None, None, :, None]
    full = jnp.broadcast_to(full, (group_count, 3, rows_ok.shape[0], group_width))
    return full.reshape(group_count, -1)


def unband(term, many_rows, group_count, group_width):
    depth = term.shape[-1]
    split = term.reshape(group_count, 3, many_rows, group_width, depth)
    total = jnp.zeros((many_rows, group_count + 2, group_width, depth), jnp.float32)
    for shift_by in range(3):
        placed = split[:, shift_by].transpose(1, 0, 2, 3)
        total = total + jnp.pad(placed, ((0, 0), (shift_by, 2 - shift_by), (0, 0), (0, 0)))
    return total[:, 1 : group_count + 1].reshape(many_rows * group_count * group_width, depth)


def query_side(q_group, o_group, k_band, v_band, mask, score_scale):
    scores = (
        jnp.einsum("gqd,gkd->gqk", q_group, k_band, preferred_element_type=jnp.float32)
        * score_scale
    )
    masked = jnp.where(mask[:, None, :], scores, -jnp.inf)
    row_max = jnp.max(masked, axis=-1, keepdims=True)
    weights = jnp.exp(masked - row_max)
    totals = jnp.sum(weights, axis=-1, keepdims=True)
    probs = weights / totals
    probs_b = probs.astype(jnp.bfloat16)
    attended = jnp.einsum(
        "gqk,gkd->gqd", probs_b, v_band, preferred_element_type=jnp.float32
    ).astype(jnp.bfloat16)
    delta = jnp.einsum("gqd,gqd->gq", o_group, attended, preferred_element_type=jnp.float32)
    grad_probs = jnp.einsum("gqd,gkd->gqk", o_group, v_band, preferred_element_type=jnp.float32)
    grad_scores = (probs * (grad_probs - delta[:, :, None]) * score_scale).astype(jnp.bfloat16)
    grad_q = jnp.einsum(
        "gqk,gkd->gqd", grad_scores, k_band, preferred_element_type=jnp.float32
    ).astype(jnp.bfloat16)
    log_total = row_max[:, :, 0] + jnp.log(totals[:, :, 0])
    grad_k_term = jnp.einsum(
        "gqk,gqd->gkd", grad_scores, q_group, preferred_element_type=jnp.float32
    )
    grad_v_term = jnp.einsum("gqk,gqd->gkd", probs_b, o_group, preferred_element_type=jnp.float32)
    return (attended, grad_q, log_total, delta, grad_k_term, grad_v_term)


def local(queries, keys, values, d_out, reach):
    frames_here, rows_here, columns, chans = queries.shape
    tok_count = frames_here * rows_here * columns
    row_count = frames_here * rows_here
    many_rows = 9 * row_count
    group_width = WT
    group_count = columns // group_width
    head_count = reach.shape[2]
    head_size = chans // head_count
    score_scale = head_size ** (-0.5)
    q_rows = queries.reshape(tok_count, chans)
    o_rows = d_out.reshape(tok_count, chans)
    k_rows = keys.reshape(tok_count, chans)
    v_rows = values.reshape(tok_count, chans)
    stacked = jnp.stack(
        [k_rows.reshape(1, 1, tok_count, chans), v_rows.reshape(1, 1, tok_count, chans)]
    )
    extended = extended_2(stacked, (("frame", 1), ("height", 2)), 1)
    k_near = extended[0].reshape(9 * tok_count, chans)
    v_near = extended[1].reshape(9 * tok_count, chans)
    frame_pos = lax.axis_index("frame")
    height_pos = lax.axis_index("height")
    frame_step = jnp.repeat(jnp.arange(3, dtype=jnp.int32) - 1, 3)
    height_step = jnp.tile(jnp.arange(3, dtype=jnp.int32) - 1, 3)
    ingrid = (frame_pos + frame_step >= 0) & (frame_pos + frame_step < lax.axis_size("frame"))
    ingrid = (
        ingrid
        & (height_pos + height_step >= 0)
        & (height_pos + height_step < lax.axis_size("height"))
    )
    reach_here = reach.reshape(head_count, 2)
    attended_list, grad_q_list, log_list, delta_list, gk_list, gv_list = ([], [], [], [], [], [])
    for head in range(head_count):
        cols = slice(head * head_size, (head + 1) * head_size)
        tile_ok = (
            ingrid
            & (jnp.abs(frame_step) <= reach_here[head, 0])
            & (jnp.abs(height_step) <= reach_here[head, 1])
        )
        mask = band_mask(jnp.repeat(tile_ok, row_count), group_count, group_width)
        q_group = to_groups(q_rows[:, cols], row_count, group_count, group_width)
        o_group = to_groups(o_rows[:, cols], row_count, group_count, group_width)
        k_band = band(k_near[:, cols].reshape(many_rows, group_count, group_width, head_size))
        v_band = band(v_near[:, cols].reshape(many_rows, group_count, group_width, head_size))
        result = query_side(q_group, o_group, k_band, v_band, mask, score_scale)
        attended_list.append(from_groups(result[0], row_count, group_count, group_width))
        grad_q_list.append(from_groups(result[1], row_count, group_count, group_width))
        log_list.append(
            from_groups(result[2][:, :, None], row_count, group_count, group_width)[:, 0]
        )
        delta_list.append(
            from_groups(result[3][:, :, None], row_count, group_count, group_width)[:, 0]
        )
        gk_list.append(unband(result[4], many_rows, group_count, group_width))
        gv_list.append(unband(result[5], many_rows, group_count, group_width))
    attended = jnp.concatenate(attended_list, axis=-1)
    grad_queries = jnp.concatenate(grad_q_list, axis=-1)
    grad_k_terms = jnp.concatenate(gk_list, axis=-1)
    grad_v_terms = jnp.concatenate(gv_list, axis=-1)
    both_terms = jnp.stack([grad_k_terms, grad_v_terms]).reshape(2, 3, 3, tok_count, chans)
    middle = both_terms[:, :, 1]
    for offset, border in ((-1, 0), (1, 2)):
        middle = middle + from_behind(
            both_terms[:, :, border].astype(jnp.bfloat16), "height", offset
        ).astype(jnp.float32)
    summed = middle[:, 1]
    for offset, border in ((-1, 0), (1, 2)):
        summed = summed + from_behind(as_sent(middle[:, border]), "frame", offset)
    grad_keys = summed[0].astype(jnp.bfloat16)
    grad_values = summed[1].astype(jnp.bfloat16)
    shape_out = (frames_here, rows_here, columns, chans)
    return (
        attended.reshape(shape_out),
        grad_queries.reshape(shape_out),
        grad_keys.reshape(shape_out),
        grad_values.reshape(shape_out),
    )


def solution(mesh):
    placed = (
        P("frame", "height", None, None),
        P("frame", "height", None, None),
        P("frame", "height", None, None),
        P("frame", "height", None, None),
        P("frame", "height", None, None),
    )
    return jax.shard_map(
        local,
        mesh=mesh,
        in_specs=placed,
        out_specs=(
            P("frame", "height", None, None),
            P("frame", "height", None, None),
            P("frame", "height", None, None),
            P("frame", "height", None, None),
        ),
        check_vma=False,
    )
```

profile of v0, /device:TPU:260, one launch (start us, length us, event | category | flops | bytes accessed | tf_op | source)
XLA Modules:
  0.0 95.2 jit_solution(8955163382311046156)
XLA Ops:
  0.7 1.0 %pad_maximum_fusion.2 = bf16[2,1,1,160,256]{4,3,2,1,0:T(8,128)(2,1)S(1)} fusion(bf16[1,1,1,160,256]{4,3,2,1,0:T(8,128)(2,1)} %bitcast.290, bf16[1,1,1,160,256]{4,3,2,1,0:T(8,128)(2,1)} %bitcast.293), kind=kLoop, calls=%fused_computation.82 | loop fusion | flops 81920 | bytes 327680 | tf_op jit(solution)/shard_map/stack | solution.py:121
  1.7 3.6 %collective-permute-start.1 = (bf16[2,1,1,160,256]{4,3,2,1,0:T(8,128)(2,1)S(1)}, bf16[2,1,1,160,256]{4,3,2,1,0:T(8,128)(2,1)S(1)}, u32[]{:S(2)}, u32[]{:S(2)}) collective-permute-start(bf16[2,1,1,160,256]{4,3,2,1,0:T(8,128)(2,1)S(1)} %pad_maximum_fusion.2), channel_id=1, source_target_pairs={{16,0},{32,16},{48,32},{64,48},{80,64},{96,80},{112,96},{128,112},... | collective-permute-start | bytes 491528 | tf_op jit(solution)/shard_map/ppermute | solution.py:17
  5.2 2.3 %collective-permute-start = (bf16[2,1,1,160,256]{4,3,2,1,0:T(8,128)(2,1)S(1)}, bf16[2,1,1,160,256]{4,3,2,1,0:T(8,128)(2,1)S(1)}, u32[]{:S(2)}, u32[]{:S(2)}) collective-permute-start(bf16[2,1,1,160,256]{4,3,2,1,0:T(8,128)(2,1)S(1)} %pad_maximum_fusion.2), channel_id=1, source_target_pairs={{0,16},{16,32},{32,48},{48,64},{64,80},{80,96},{96,112},{112,128},... | collective-permute-start | bytes 491528 | tf_op jit(solution)/shard_map/ppermute | solution.py:16
  7.5 1.4 %fusion.81 = (s32[1,1]{1,0:T(1,128)}, s32[1,1]{1,0:T(1,128)}, s32[1,1]{1,0:T(1,128)}, s32[1,1]{1,0:T(1,128)}) fusion(s32[2,2]{1,0:T(2,128)} %bitcast.312), kind=kLoop, calls=%fused_computation.148 | loop fusion | bytes 32 | tf_op jit(solution)/shard_map/slice | solution.py:143
  9.0 0.7 broadcast_compare_fusion.3
  9.6 0.7 compare_and_fusion
  10.3 1.3 %broadcast_compare_fusion.1 = (pred[3]{0:T(512)(128)(4,1)S(1)}, pred[3]{0:T(512)(128)(4,1)S(1)}) fusion(s32[]{:T(128)} %bitcast.27, s32[]{:T(128)} %bitcast.2), kind=kLoop, calls=%fused_computation.133 | loop fusion | flops 12 | bytes 14 | tf_op jit(solution)/shard_map/le | solution.py:143
  12.2 8.9 %collective-permute-done = bf16[2,1,1,160,256]{4,3,2,1,0:T(8,128)(2,1)S(1)} collective-permute-done((bf16[2,1,1,160,256]{4,3,2,1,0:T(8,128)(2,1)S(1)}, bf16[2,1,1,160,256]{4,3,2,1,0:T(8,128)(2,1)S(1)}, u32[]{:S(2)}, u32[]{:S(2)}) %collective-permute-start) | collective-permute-done | bytes 163872 | tf_op jit(solution)/shard_map/ppermute | solution.py:16
  21.1 1.0 %pad_maximum_fusion.1 = bf16[2,3,1,160,256]{4,3,2,1,0:T(8,128)(2,1)S(1)} fusion(bf16[2,1,1,160,256]{4,3,2,1,0:T(8,128)(2,1)S(1)} %collective-permute-done.1, bf16[1,1,1,160,256]{4,3,2,1,0:T(8,128)(2,1)} %bitcast.291, bf16[1,1,1,160,256]{4,3,2,1,0:T(8,128)(2,1)} %bitcast.294, bf16[2,1,1,160,256]{4,3,2,1,0:T(8,128)(2,1)S(1)} %collective-permute-done), kind=kLoop, calls=%fused_computation.59 | loop fusion | flops 737280 | bytes 983040 | tf_op jit(solution)/shard_map/concatenate | solution.py:18
  22.1 1.9 %collective-permute-start.3 = (bf16[2,3,1,160,256]{4,3,2,1,0:T(8,128)(2,1)S(1)}, bf16[2,3,1,160,256]{4,3,2,1,0:T(8,128)(2,1)S(1)}, u32[]{:S(2)}, u32[]{:S(2)}) collective-permute-start(bf16[2,3,1,160,256]{4,3,2,1,0:T(8,128)(2,1)S(1)} %pad_maximum_fusion.1), channel_id=1, source_target_pairs={{1,0},{2,1},{3,2},{4,3},{5,4},{6,5},{7,6},{8,7},{9,8},{10,9},{11,1... | collective-permute-start | bytes 1474568 | tf_op jit(solution)/shard_map/ppermute | solution.py:17
  24.0 2.4 %collective-permute-start.2 = (bf16[2,3,1,160,256]{4,3,2,1,0:T(8,128)(2,1)S(1)}, bf16[2,3,1,160,256]{4,3,2,1,0:T(8,128)(2,1)S(1)}, u32[]{:S(2)}, u32[]{:S(2)}) collective-permute-start(bf16[2,3,1,160,256]{4,3,2,1,0:T(8,128)(2,1)S(1)} %pad_maximum_fusion.1), channel_id=1, source_target_pairs={{0,1},{1,2},{2,3},{3,4},{4,5},{5,6},{6,7},{7,8},{8,9},{9,10},{10,1... | collective-permute-start | bytes 1474568 | tf_op jit(solution)/shard_map/ppermute | solution.py:16
  27.2 5.5 %collective-permute-done.3 = bf16[2,3,1,160,256]{4,3,2,1,0:T(8,128)(2,1)S(1)} collective-permute-done((bf16[2,3,1,160,256]{4,3,2,1,0:T(8,128)(2,1)S(1)}, bf16[2,3,1,160,256]{4,3,2,1,0:T(8,128)(2,1)S(1)}, u32[]{:S(2)}, u32[]{:S(2)}) %collective-permute-start.3) | collective-permute-done | bytes 491552 | tf_op jit(solution)/shard_map/ppermute | solution.py:17
  32.6 4.9 %collective-permute-done.2 = bf16[2,3,1,160,256]{4,3,2,1,0:T(8,128)(2,1)S(1)} collective-permute-done((bf16[2,3,1,160,256]{4,3,2,1,0:T(8,128)(2,1)S(1)}, bf16[2,3,1,160,256]{4,3,2,1,0:T(8,128)(2,1)S(1)}, u32[]{:S(2)}, u32[]{:S(2)}) %collective-permute-start.2) | collective-permute-done | bytes 491552 | tf_op jit(solution)/shard_map/ppermute | solution.py:16
  37.8 0.8 fusion.77
  38.6 0.8 fusion.76
  39.6 0.2 copy.29
  39.8 0.5 fusion.13
  40.4 1.7 %fusion.82 = (f32[10,16]{1,0:T(8,128)S(1)}, f32[10,16,432]{2,1,0:T(8,128)S(1)}) fusion(f32[10,16,432]{2,1,0:T(8,128)S(1)} %fusion.13), kind=kOutput, calls=%fused_computation.149 | output fusion | flops 138671 | bytes 553600 | tf_op jit(solution)/shard_map/sub | solution.py:86
  42.3 0.2 copy.31
  42.5 2.1 %fusion.37 = f32[10,432,128]{2,1,0:T(8,128)} fusion(bf16[10,2,8,128]{3,2,0,1:T(8,128)(2,1)S(1)} %bitcast.305, f32[10,16]{1,0:T(8,128)S(1)} %get-tuple-element.50, f32[10,16,432]{2,1,0:T(8,128)S(1)} %fusion.13), kind=kOutput, calls=%fused_computation.93 | convolution fusion | flops 17902672 | bytes 2529920 | tf_op jit(solution)/shard_map/gqk,gqd->gkd/dot_general | solution.py:103
  44.7 0.5 fusion.35
  45.1 0.6 fusion.17
  45.7 0.3 fusion.19
  46.0 0.5 fusion.43
  46.6 0.5 copy-done.2
  47.5 0.5 fusion.15
  48.0 0.9 fusion.83
  49.1 1.2 %copy.27 = bf16[10,3,18,8,128]{4,3,2,1,0:T(8,128)(2,1)} copy(bf16[10,3,18,8,128]{4,3,0,2,1:T(8,128)(2,1)S(1)} %maximum_bitcast_fusion.1) | data formatting | bytes 2211840 | tf_op jit(solution)/shard_map/transpose | solution.py:54
  50.3 3.2 %fusion.40 = f32[10,432,128]{2,1,0:T(8,128)} fusion(bf16[10,2,8,128]{3,2,0,1:T(8,128)(2,1)S(1)} %bitcast.302, f32[10,16]{1,0:T(8,128)S(1)} %get-tuple-element.52, f32[10,16,432]{2,1,0:T(8,128)} %copy-done.3), kind=kOutput, calls=%fused_computation.96 | convolution fusion | flops 17902672 | bytes 2529920 | tf_op jit(solution)/shard_map/gqk,gqd->gkd/dot_general | solution.py:103
  53.5 1.9 %fusion.36 = (f32[10,16]{1,0:T(8,128)S(1)}, bf16[10,16,128]{2,1,0:T(8,128)(2,1)S(1)}) fusion(bf16[10,2,8,128]{3,2,0,1:T(8,128)(2,1)S(1)} %bitcast.303, bf16[10,432,128]{2,1,0:T(8,128)(2,1)} %bitcast.286, f32[10,16]{1,0:T(8,128)S(1)} %get-tuple-element.52, f32[10,16,432]{2,1,0:T(8,128)} %copy-done.3), kind=kOutput, calls=%fused_computation.92 | convolution fusion | flops 18004912 | bytes 1465600 | tf_op jit(solution)/shard_map/gqk,gkd->gqd/dot_general | solution.py:90
  55.4 1.7 %fusion.73 = (f32[10,1,18,8,128]{4,3,2,1,0:T(8,128)S(1)}, f32[10,1,18,8,128]{4,3,2,1,0:T(8,128)S(1)}, f32[10,1,18,8,128]{4,3,2,1,0:T(8,128)S(1)}) fusion(f32[10,3,18,8,128]{4,3,2,1,0:T(8,128)} %bitcast.254), kind=kLoop, calls=%fused_computation.140 | loop fusion | bytes 4423680 | tf_op jit(solution)/shard_map/slice | solution.py:74
  57.3 1.5 %copy-done = f32[10,432,128]{2,1,0:T(8,128)S(1)} copy-done((f32[10,432,128]{2,1,0:T(8,128)S(1)}, f32[10,432,128]{2,1,0:T(8,128)}, u32[]{:S(2)}) %copy-start) | copy-done | bytes 2211864
  59.2 1.2 %copy-done.4 = bf16[10,3,18,8,128]{4,3,2,1,0:T(8,128)(2,1)S(1)} copy-done((bf16[10,3,18,8,128]{4,3,2,1,0:T(8,128)(2,1)S(1)}, bf16[10,3,18,8,128]{4,3,2,1,0:T(8,128)(2,1)}, u32[]{:S(2)}) %copy-start.4) | copy-done | bytes 1105944
  60.4 0.5 fusion.16
  61.0 0.5 fusion.46
  62.8 0.2 maximum_maximum_fusion
  63.0 1.9 %collective-permute-start.4 = (bf16[2,3,160,256]{3,2,1,0:T(8,128)(2,1)S(1)}, bf16[2,3,160,256]{3,2,1,0:T(8,128)(2,1)S(1)}, u32[]{:S(2)}, u32[]{:S(2)}) collective-permute-start(bf16[2,3,160,256]{3,2,1,0:T(8,128)(2,1)S(1)} %get-tuple-element.18), channel_id=1, source_target_pairs={{1,0},{2,1},{3,2},{4,3},{5,4},{6,5},{7,6},{8,7},{9,8},{10,9},{11,1... | collective-permute-start | bytes 1474568 | tf_op jit(solution)/shard_map/ppermute | solution.py:25
  65.0 2.4 %collective-permute-start.5 = (bf16[2,3,160,256]{3,2,1,0:T(8,128)(2,1)S(1)}, bf16[2,3,160,256]{3,2,1,0:T(8,128)(2,1)S(1)}, u32[]{:S(2)}, u32[]{:S(2)}) collective-permute-start(bf16[2,3,160,256]{3,2,1,0:T(8,128)(2,1)S(1)} %get-tuple-element.19), channel_id=1, source_target_pairs={{0,1},{1,2},{2,3},{3,4},{4,5},{5,6},{6,7},{7,8},{8,9},{9,10},{10,1... | collective-permute-start | bytes 1474568 | tf_op jit(solution)/shard_map/ppermute | solution.py:25
  67.4 0.3 fusion.18
  67.7 6.9 %collective-permute-done.4 = bf16[2,3,160,256]{3,2,1,0:T(8,128)(2,1)S(1)} collective-permute-done((bf16[2,3,160,256]{3,2,1,0:T(8,128)(2,1)S(1)}, bf16[2,3,160,256]{3,2,1,0:T(8,128)(2,1)S(1)}, u32[]{:S(2)}, u32[]{:S(2)}) %collective-permute-start.4) | collective-permute-done | bytes 491552 | tf_op jit(solution)/shard_map/ppermute | solution.py:25
  74.6 2.9 %collective-permute-done.5 = bf16[2,3,160,256]{3,2,1,0:T(8,128)(2,1)S(1)} collective-permute-done((bf16[2,3,160,256]{3,2,1,0:T(8,128)(2,1)S(1)}, bf16[2,3,160,256]{3,2,1,0:T(8,128)(2,1)S(1)}, u32[]{:S(2)}, u32[]{:S(2)}) %collective-permute-start.5) | collective-permute-done | bytes 491552 | tf_op jit(solution)/shard_map/ppermute | solution.py:25
  77.5 0.2 fusion.69
  77.8 1.9 %collective-permute-start.6 = (bf16[2,160,256]{2,1,0:T(8,128)(2,1)S(1)}, bf16[2,160,256]{2,1,0:T(8,128)(2,1)S(1)}, u32[]{:S(2)}, u32[]{:S(2)}) collective-permute-start(bf16[2,160,256]{2,1,0:T(8,128)(2,1)S(1)} %get-tuple-element.26), channel_id=1, source_target_pairs={{16,0},{32,16},{48,32},{64,48},{80,64},{96,80},{112,96},{128,112},... | collective-permute-start | bytes 491528 | tf_op jit(solution)/shard_map/ppermute | solution.py:25
  79.7 3.9 %collective-permute-start.7 = (bf16[2,160,256]{2,1,0:T(8,128)(2,1)S(1)}, bf16[2,160,256]{2,1,0:T(8,128)(2,1)S(1)}, u32[]{:S(2)}, u32[]{:S(2)}) collective-permute-start(bf16[2,160,256]{2,1,0:T(8,128)(2,1)S(1)} %get-tuple-element.27), channel_id=1, source_target_pairs={{0,16},{16,32},{32,48},{48,64},{64,80},{80,96},{96,112},{112,128},... | collective-permute-start | bytes 491528 | tf_op jit(solution)/shard_map/ppermute | solution.py:25
  83.6 0.6 pad_maximum_fusion.4
  84.3 0.6 pad_maximum_fusion.3
  85.0 9.5 %collective-permute-done.7 = bf16[2,160,256]{2,1,0:T(8,128)(2,1)S(1)} collective-permute-done((bf16[2,160,256]{2,1,0:T(8,128)(2,1)S(1)}, bf16[2,160,256]{2,1,0:T(8,128)(2,1)S(1)}, u32[]{:S(2)}, u32[]{:S(2)}) %collective-permute-start.7) | collective-permute-done | bytes 163872 | tf_op jit(solution)/shard_map/ppermute | solution.py:25
  94.5 0.7 fusion.78
  (73 shorter events, 4.6 us)
Async XLA Ops:
  0.6 36.9 %copy-start.5 = (bf16[1,2,80,256]{3,2,1,0:T(8,128)(2,1)S(1)}, bf16[1,2,80,256]{3,2,1,0:T(8,128)(2,1)}, u32[]{:S(2)}) copy-start(bf16[1,2,80,256]{3,2,1,0:T(8,128)(2,1)} %param.7) | copy-start | bytes 245764
  0.6 36.9 %copy-start.6 = (bf16[1,2,80,256]{3,2,1,0:T(8,128)(2,1)S(1)}, bf16[1,2,80,256]{3,2,1,0:T(8,128)(2,1)}, u32[]{:S(2)}) copy-start(bf16[1,2,80,256]{3,2,1,0:T(8,128)(2,1)} %param.6) | copy-start | bytes 245764
  0.7 26.5 %copy-start.8 = (bf16[1,2,80,256]{3,2,1,0:T(8,128)(2,1)S(1)}, bf16[1,2,80,256]{3,2,1,0:T(8,128)(2,1)}, u32[]{:S(2)}) copy-start(bf16[1,2,80,256]{3,2,1,0:T(8,128)(2,1)} %param.5) | copy-start | bytes 245764
  0.7 26.5 %copy-start.9 = (bf16[1,2,80,256]{3,2,1,0:T(8,128)(2,1)S(1)}, bf16[1,2,80,256]{3,2,1,0:T(8,128)(2,1)}, u32[]{:S(2)}) copy-start(bf16[1,2,80,256]{3,2,1,0:T(8,128)(2,1)} %param.8) | copy-start | bytes 245764
  1.7 10.5 %collective-permute-start.1 = (bf16[2,1,1,160,256]{4,3,2,1,0:T(8,128)(2,1)S(1)}, bf16[2,1,1,160,256]{4,3,2,1,0:T(8,128)(2,1)S(1)}, u32[]{:S(2)}, u32[]{:S(2)}) collective-permute-start(bf16[2,1,1,160,256]{4,3,2,1,0:T(8,128)(2,1)S(1)} %pad_maximum_fusion.2), channel_id=1, source_target_pairs={{16,0},{32,16},{48,32},{64,48},{80,64},{96,80},{112,96},{128,112},... | collective-permute-start | bytes 491528 | tf_op jit(solution)/shard_map/ppermute | solution.py:17
  5.2 15.8 %collective-permute-start = (bf16[2,1,1,160,256]{4,3,2,1,0:T(8,128)(2,1)S(1)}, bf16[2,1,1,160,256]{4,3,2,1,0:T(8,128)(2,1)S(1)}, u32[]{:S(2)}, u32[]{:S(2)}) collective-permute-start(bf16[2,1,1,160,256]{4,3,2,1,0:T(8,128)(2,1)S(1)} %pad_maximum_fusion.2), channel_id=1, source_target_pairs={{0,16},{16,32},{32,48},{48,64},{64,80},{80,96},{96,112},{112,128},... | collective-permute-start | bytes 491528 | tf_op jit(solution)/shard_map/ppermute | solution.py:16
  22.1 10.6 %collective-permute-start.3 = (bf16[2,3,1,160,256]{4,3,2,1,0:T(8,128)(2,1)S(1)}, bf16[2,3,1,160,256]{4,3,2,1,0:T(8,128)(2,1)S(1)}, u32[]{:S(2)}, u32[]{:S(2)}) collective-permute-start(bf16[2,3,1,160,256]{4,3,2,1,0:T(8,128)(2,1)S(1)} %pad_maximum_fusion.1), channel_id=1, source_target_pairs={{1,0},{2,1},{3,2},{4,3},{5,4},{6,5},{7,6},{8,7},{9,8},{10,9},{11,1... | collective-permute-start | bytes 1474568 | tf_op jit(solution)/shard_map/ppermute | solution.py:17
  24.0 13.5 %collective-permute-start.2 = (bf16[2,3,1,160,256]{4,3,2,1,0:T(8,128)(2,1)S(1)}, bf16[2,3,1,160,256]{4,3,2,1,0:T(8,128)(2,1)S(1)}, u32[]{:S(2)}, u32[]{:S(2)}) collective-permute-start(bf16[2,3,1,160,256]{4,3,2,1,0:T(8,128)(2,1)S(1)} %pad_maximum_fusion.1), channel_id=1, source_target_pairs={{0,1},{1,2},{2,3},{3,4},{4,5},{5,6},{6,7},{7,8},{8,9},{9,10},{10,1... | collective-permute-start | bytes 1474568 | tf_op jit(solution)/shard_map/ppermute | solution.py:16
  46.0 1.0 %copy-start.2 = (bf16[1440,128]{1,0:T(8,128)(2,1)S(1)}, bf16[1440,128]{1,0:T(8,128)(2,1)}, u32[]{:S(2)}) copy-start(bf16[1440,128]{1,0:T(8,128)(2,1)} %get-tuple-element.22) | copy-start | bytes 1105924
  47.4 1.4 %copy-start.1 = (bf16[1440,128]{1,0:T(8,128)(2,1)S(1)}, bf16[1440,128]{1,0:T(8,128)(2,1)}, u32[]{:S(2)}) copy-start(bf16[1440,128]{1,0:T(8,128)(2,1)} %get-tuple-element.24) | copy-start | bytes 1105924
  48.0 1.0 %copy-start.3 = (f32[10,16,432]{2,1,0:T(8,128)}, f32[10,16,432]{2,1,0:T(8,128)S(1)}, u32[]{:S(2)}) copy-start(f32[10,16,432]{2,1,0:T(8,128)S(1)} %fusion.15) | copy-start | bytes 829444
  57.2 1.6 %copy-start = (f32[10,432,128]{2,1,0:T(8,128)S(1)}, f32[10,432,128]{2,1,0:T(8,128)}, u32[]{:S(2)}) copy-start(f32[10,432,128]{2,1,0:T(8,128)} %fusion.37) | copy-start | bytes 6635524
  59.1 1.2 %copy-start.4 = (bf16[10,3,18,8,128]{4,3,2,1,0:T(8,128)(2,1)S(1)}, bf16[10,3,18,8,128]{4,3,2,1,0:T(8,128)(2,1)}, u32[]{:S(2)}) copy-start(bf16[10,3,18,8,128]{4,3,2,1,0:T(8,128)(2,1)} %copy.27) | copy-start | bytes 3317764
  59.1 1.3 %copy-start.7 = (f32[10,16,432]{2,1,0:T(8,128)S(1)}, f32[10,16,432]{2,1,0:T(8,128)}, u32[]{:S(2)}) copy-start(f32[10,16,432]{2,1,0:T(8,128)} %get-tuple-element.53) | copy-start | bytes 829444
  63.0 11.6 %collective-permute-start.4 = (bf16[2,3,160,256]{3,2,1,0:T(8,128)(2,1)S(1)}, bf16[2,3,160,256]{3,2,1,0:T(8,128)(2,1)S(1)}, u32[]{:S(2)}, u32[]{:S(2)}) collective-permute-start(bf16[2,3,160,256]{3,2,1,0:T(8,128)(2,1)S(1)} %get-tuple-element.18), channel_id=1, source_target_pairs={{1,0},{2,1},{3,2},{4,3},{5,4},{6,5},{7,6},{8,7},{9,8},{10,9},{11,1... | collective-permute-start | bytes 1474568 | tf_op jit(solution)/shard_map/ppermute | solution.py:25
  65.0 12.6 %collective-permute-start.5 = (bf16[2,3,160,256]{3,2,1,0:T(8,128)(2,1)S(1)}, bf16[2,3,160,256]{3,2,1,0:T(8,128)(2,1)S(1)}, u32[]{:S(2)}, u32[]{:S(2)}) collective-permute-start(bf16[2,3,160,256]{3,2,1,0:T(8,128)(2,1)S(1)} %get-tuple-element.19), channel_id=1, source_target_pairs={{0,1},{1,2},{2,3},{3,4},{4,5},{5,6},{6,7},{7,8},{8,9},{9,10},{10,1... | collective-permute-start | bytes 1474568 | tf_op jit(solution)/shard_map/ppermute | solution.py:25
  77.8 7.2 %collective-permute-start.6 = (bf16[2,160,256]{2,1,0:T(8,128)(2,1)S(1)}, bf16[2,160,256]{2,1,0:T(8,128)(2,1)S(1)}, u32[]{:S(2)}, u32[]{:S(2)}) collective-permute-start(bf16[2,160,256]{2,1,0:T(8,128)(2,1)S(1)} %get-tuple-element.26), channel_id=1, source_target_pairs={{16,0},{32,16},{48,32},{64,48},{80,64},{96,80},{112,96},{128,112},... | collective-permute-start | bytes 491528 | tf_op jit(solution)/shard_map/ppermute | solution.py:25
  79.7 14.7 %collective-permute-start.7 = (bf16[2,160,256]{2,1,0:T(8,128)(2,1)S(1)}, bf16[2,160,256]{2,1,0:T(8,128)(2,1)S(1)}, u32[]{:S(2)}, u32[]{:S(2)}) collective-permute-start(bf16[2,160,256]{2,1,0:T(8,128)(2,1)S(1)} %get-tuple-element.27), channel_id=1, source_target_pairs={{0,16},{16,32},{32,48},{48,64},{64,80},{80,96},{96,112},{112,128},... | collective-permute-start | bytes 491528 | tf_op jit(solution)/shard_map/ppermute | solution.py:25
where the time goes:
time: 95.8 us; the launch traced here: 95.2 us
  waiting for transfers between devices  38.5 us (40%)
  starting transfers between devices  20.3 us (21%)
  local copies, waits for them, and re-layouts  13.3 us (14%)
  matrix products  11.5 us (12%)
  other arithmetic  10.3 us (11%)
  between operations  1.22 us (1%)
    ppermute x4, waiting for transfers between devices, from_behind(): return lax.ppermute(shard, axis, pairs)  19.3 us
    ppermute x2, waiting for transfers between devices, extended_2(): before = lax.ppermute(last, axis, up)  13.7 us
    ppermute x4, starting transfers between devices, from_behind(): return lax.ppermute(shard, axis, pairs)  10.2 us
    ppermute x2, starting transfers between devices, extended_2(): after = lax.ppermute(first, axis, down)  5.48 us
    ppermute x2, waiting for transfers between devices, extended_2(): after = lax.ppermute(first, axis, down)  5.45 us
    dot_general x2, matrix products, query_side(): jnp.einsum('gqk,gqd->gkd', probs_b, o_group, preferred_element_type=jnp.f...  5.33 us
    ppermute x2, starting transfers between devices, extended_2(): before = lax.ppermute(last, axis, up)  4.69 us
    unnamed x32, local copies, waits for them, and re-layouts  3.82 us
  transfers between devices with their start and end apart: 8, of which 7 were waited for; matrix products, arithmetic and copies ran while one was open for 7% of the time, Pallas kernels for 0%

commit v1 on v0

v1 whole, which is shorter than its diff:
```python
import functools

import jax
import jax.numpy as jnp
from jax import lax
from jax.experimental import pallas as pl
from jax.experimental.pallas import tpu as pltpu
from jax.sharding import PartitionSpec as P

W = 80
WT = 8
GROUPS = W // WT
TOK = 160
HEADS = 2
HD = 128
CHANS = HEADS * HD
BLOCKS = W // 16
SPAN = 288
KEYS = 1440
PADDED = 1536
TILE = 256
NEG = -1e30
LOG2E = 1.4426950408889634
BOTH = ("frame", "height")


def tile_groups():
    found = []
    for m in range(PADDED // TILE):
        lo, hi = m * TILE, min((m + 1) * TILE, KEYS)
        first, last = lo // SPAN, (hi - 1) // SPAN
        found.append((max(2 * first - 1, 0), min(2 * last + 2, GROUPS - 1)))
    return found


TILE_GROUPS = tile_groups()
GROUP_TILES = [
    [m for m, (a, b) in enumerate(TILE_GROUPS) if a <= g <= b] for g in range(GROUPS)
]


def dot_nt(a, b):
    return lax.dot_general(a, b, (((1,), (1,)), ((), ())), preferred_element_type=jnp.float32)


def dot_nn(a, b):
    return lax.dot_general(a, b, (((1,), (0,)), ((), ())), preferred_element_type=jnp.float32)


def dot_tn(a, b):
    return lax.dot_general(a, b, (((0,), (0,)), ((), ())), preferred_element_type=jnp.float32)


def by_group(ref):
    wide = ref[...].astype(jnp.float32)
    parts = []
    for g in range(GROUPS):
        for r in range(2):
            parts.append(wide[r * W + g * WT : r * W + (g + 1) * WT])
    return jnp.concatenate(parts, axis=0).astype(jnp.bfloat16)


def by_row(wide):
    parts = []
    for r in range(2):
        for g in range(GROUPS):
            parts.append(wide[g * 16 + r * WT : g * 16 + (r + 1) * WT])
    return jnp.concatenate(parts, axis=0).astype(jnp.bfloat16)


def attn_kernel(
    nframe, nheight,
    reach, q, o, x, xe, xf, xo, xeo, xfo, xp,
    att, gq, ge, geo, gfo_, go, gfe, gfo, gown,
    qs, os_, ks, vs, sc, dp, pb, ds, gk, gv, aacc, qacc,
):
    frame, height = lax.axis_index("frame"), lax.axis_index("height")
    fo_ok = (frame > 0) & (frame < nframe - 1)
    o_ok = (height > 0) & (height < nheight - 1)
    slots = [(x, 0), (xp, 0), (xo, 0), (xe, 0), (xp, 2), (xeo, 0), (xf, 0), (xp, 4), (xfo, 0)]
    for slot, (ref, at) in enumerate(slots):
        for j in range(BLOCKS):
            for r in range(2):
                row = j * SPAN + (slot * 2 + r) * 16
                src = slice(r * W + 16 * j, r * W + 16 * j + 16)
                ks[row : row + 16] = ref[at, src]
                vs[row : row + 16] = ref[at + 1, src]
    ks[KEYS:] = jnp.zeros((PADDED - KEYS, CHANS), jnp.bfloat16)
    vs[KEYS:] = jnp.zeros((PADDED - KEYS, CHANS), jnp.bfloat16)
    qs[...] = by_group(q)
    os_[...] = by_group(o)

    key = lax.broadcasted_iota(jnp.int32, (1, PADDED), 1)
    block = key // SPAN
    within = key - block * SPAN
    key_row = within // 16
    key_group = jnp.where(key < KEYS, block * 2 + (within % 16) // WT, 1000)
    slot_of = key_row // 2
    a_of, b_of = slot_of // 3, slot_of % 3

    scale = HD ** (-0.5)
    for h in range(HEADS):
        hs = slice(h * HD, (h + 1) * HD)
        frames = reach[0, 0, h, 0] > 0
        rows = reach[0, 0, h, 1] > 0
        zero, neg = jnp.float32(0), jnp.float32(NEG)
        fe_b = jnp.where(frames, zero, neg)
        fo_b = jnp.where(frames & fo_ok, zero, neg)
        p_b = jnp.where(rows, zero, neg)
        o_b = jnp.where(rows & o_ok, zero, neg)
        ok = jnp.where(a_of == 1, fe_b, jnp.where(a_of == 2, fo_b, zero))
        ok = jnp.minimum(ok, jnp.where(b_of == 1, p_b, jnp.where(b_of == 2, o_b, zero)))
        for m, (a, b) in enumerate(TILE_GROUPS):
            qr, kr = slice(a * 16, (b + 1) * 16), slice(m * TILE, (m + 1) * TILE)
            sc[qr, kr] = dot_nt(qs[qr, hs], ks[kr, hs])
            dp[qr, kr] = dot_nt(os_[qr, hs], vs[kr, hs])
        for g in range(GROUPS):
            qr = slice(g * 16, (g + 1) * 16)
            kr = slice(GROUP_TILES[g][0] * TILE, (GROUP_TILES[g][-1] + 1) * TILE)
            bias = jnp.where(jnp.abs(key_group[:, kr] - g) <= 1, ok[:, kr], NEG)
            s = sc[qr, kr] * (scale * LOG2E) + bias
            e = jnp.exp2(s - jnp.max(s, axis=1, keepdims=True))
            p = e * (1.0 / jnp.sum(e, axis=1, keepdims=True))
            d = dp[qr, kr]
            delta = jnp.sum(p * d, axis=1, keepdims=True)
            pb[qr, kr] = p.astype(jnp.bfloat16)
            ds[qr, kr] = (p * ((d - delta) * scale)).astype(jnp.bfloat16)
        aacc[...] = jnp.zeros_like(aacc)
        qacc[...] = jnp.zeros_like(qacc)
        for m, (a, b) in enumerate(TILE_GROUPS):
            qr, kr = slice(a * 16, (b + 1) * 16), slice(m * TILE, (m + 1) * TILE)
            pt, dt = pb[qr, kr], ds[qr, kr]
            gv[kr, hs] = dot_tn(pt, os_[qr, hs])
            gk[kr, hs] = dot_tn(dt, qs[qr, hs])
            aacc[qr] += dot_nn(pt, vs[kr, hs])
            qacc[qr] += dot_nn(dt, ks[kr, hs])
        att[:, hs] = by_row(aacc[...])
        gq[:, hs] = by_row(qacc[...])
    outs = [(gown, 0), (ge, 0), (go, 0), (gfe, 0), (ge, 2), (geo, 0), (gfo, 0), (ge, 4), (gfo_, 0)]
    for slot, (ref, at) in enumerate(outs):
        for j in range(BLOCKS):
            for r in range(2):
                row = j * SPAN + (slot * 2 + r) * 16
                dst = slice(r * W + 16 * j, r * W + 16 * j + 16)
                ref[at, dst] = gk[row : row + 16].astype(ref.dtype)
                ref[at + 1, dst] = gv[row : row + 16].astype(ref.dtype)


def attention(reach, q, o, x, xe, xf, xo, xeo, xfo, xp):
    nframe, nheight = lax.axis_size("frame"), lax.axis_size("height")
    vmem = pl.BlockSpec(memory_space=pltpu.VMEM)
    bf = lambda *shape: jax.ShapeDtypeStruct(shape, jnp.bfloat16)
    fl = lambda *shape: jax.ShapeDtypeStruct(shape, jnp.float32)
    pair = (2, TOK, CHANS)
    return pl.pallas_call(
        functools.partial(attn_kernel, nframe, nheight),
        out_shape=(
            bf(TOK, CHANS), bf(TOK, CHANS), bf(6, TOK, CHANS), bf(*pair), bf(*pair),
            fl(*pair), fl(*pair), fl(*pair), fl(*pair),
        ),
        in_specs=[pl.BlockSpec(memory_space=pltpu.SMEM)] + [vmem] * 9,
        out_specs=(vmem,) * 9,
        scratch_shapes=[
            pltpu.VMEM((TOK, CHANS), jnp.bfloat16),
            pltpu.VMEM((TOK, CHANS), jnp.bfloat16),
            pltpu.VMEM((PADDED, CHANS), jnp.bfloat16),
            pltpu.VMEM((PADDED, CHANS), jnp.bfloat16),
            pltpu.VMEM((TOK, PADDED), jnp.float32),
            pltpu.VMEM((TOK, PADDED), jnp.float32),
            pltpu.VMEM((TOK, PADDED), jnp.bfloat16),
            pltpu.VMEM((TOK, PADDED), jnp.bfloat16),
            pltpu.VMEM((PADDED, CHANS), jnp.float32),
            pltpu.VMEM((PADDED, CHANS), jnp.float32),
            pltpu.VMEM((TOK, HD), jnp.float32),
            pltpu.VMEM((TOK, HD), jnp.float32),
        ],
        compiler_params=pltpu.CompilerParams(vmem_limit_bytes=48 * 1024 * 1024),
        cost_estimate=pl.CostEstimate(
            flops=10 * 160 * 640 * 256, bytes_accessed=4 * 1024 * 1024, transcendentals=160 * 1440
        ),
        name="attention",
    )(reach, q, o, x, xe, xf, xo, xeo, xfo, xp)


def swaps():
    nf, nh = lax.axis_size("frame"), lax.axis_size("height")
    even = lambda i: i ^ 1
    odd = lambda i: ((i + 1) ^ 1) - 1
    along_f = lambda to: [
        (f * nh + h, to(f) * nh + h) for f in range(nf) for h in range(nh) if 0 <= to(f) < nf
    ]
    along_h = lambda to: [
        (f * nh + h, f * nh + to(h)) for f in range(nf) for h in range(nh) if 0 <= to(h) < nh
    ]
    return along_f(even), along_f(odd), along_h(even), along_h(odd)


def local(queries, keys, values, d_out, reach):
    fe, fo, he, ho = swaps()
    swap = lambda array, pairs: lax.ppermute(array, BOTH, pairs)
    shape = queries.shape
    q, o = queries.reshape(TOK, CHANS), d_out.reshape(TOK, CHANS)
    x = jnp.stack([keys.reshape(TOK, CHANS), values.reshape(TOK, CHANS)])
    xo = swap(x, ho)
    xf = swap(x, fo)
    xe = swap(x, fe)
    xfo = swap(xo, fo)
    xeo = swap(xo, fe)
    xp = swap(jnp.concatenate([x, xe, xf]), he)
    att, gq, ge, geo, gfo_, go, gfe, gfo, gown = attention(
        reach, q, o, x, xe, xf, xo, xeo, xfo, xp
    )
    f32, bf16 = jnp.float32, jnp.bfloat16
    rp = swap(ge, he).astype(f32)
    rfo = swap(gfo_, fo).astype(f32)
    reo = swap(geo, fe).astype(f32)
    rf = swap((gfo + rp[4:6]).astype(bf16), fo).astype(f32)
    re = swap((gfe + rp[2:4]).astype(bf16), fe).astype(f32)
    ro = swap((go + rfo + reo).astype(bf16), ho).astype(f32)
    total = (gown + rp[0:2] + rf + re + ro).astype(bf16)
    return (
        att.reshape(shape), gq.reshape(shape), total[0].reshape(shape), total[1].reshape(shape)
    )


def solution(mesh):
    spec = P("frame", "height", None, None)
    return jax.shard_map(
        local, mesh=mesh, in_specs=(spec,) * 5, out_specs=(spec,) * 4, check_vma=False
    )
```

time: 95.8 us -> 83.7 us (0.87)
  the two profiles are of different devices: /device:TPU:260 before, /device:TPU:189 now
where the time goes in v1:
time: 83.7 us; the launch traced here: 83.2 us
  starting transfers between devices  48.4 us (58%)
  waiting for transfers between devices  28.1 us (34%)
  Pallas kernels  3.29 us (4%)
  other arithmetic  1.37 us (2%)
  local copies, waits for them, and re-layouts  1.36 us (2%)
    ppermute x12, starting transfers between devices, local(): swap = lambda array, pairs: lax.ppermute(array, BOTH, pairs)  48.4 us
    ppermute x12, waiting for transfers between devices, local(): swap = lambda array, pairs: lax.ppermute(array, BOTH, pairs)  28.1 us
    pallas_call x1, Pallas kernels, attention(): pl.pallas_call(functools.partial(attn_kernel, nframe, nheight), out_shape...  3.29 us
  transfers between devices with their start and end apart: 12, of which 8 were waited for; matrix products, arithmetic and copies ran while one was open for 0% of the time, Pallas kernels for 0%

profile of v1, /device:TPU:189, one launch (start us, length us, event | category | flops | bytes accessed | tf_op | source)
XLA Modules:
  0.0 83.2 jit_solution(122089278546551614)
XLA Ops:
  0.6 0.0 copy-start.3
  0.6 0.0 copy-start.4
  0.7 1.0 %pad_maximum_fusion.1.x = bf16[2,160,256]{2,1,0:T(8,128)(2,1)S(1)} fusion(bf16[1,160,256]{2,1,0:T(8,128)(2,1)} %bitcast.10, bf16[1,160,256]{2,1,0:T(8,128)(2,1)} %bitcast.12), kind=kLoop, calls=%fused_computation.11 | loop fusion | flops 81920 | bytes 327680 | tf_op jit(solution)/shard_map/stack | solution.py:203
  1.6 0.0 copy-start
  1.6 0.0 copy-start.1
  1.7 6.4 %collective-permute-start.1 = (bf16[2,160,256]{2,1,0:T(8,128)(2,1)S(1)}, bf16[2,160,256]{2,1,0:T(8,128)(2,1)S(1)}, u32[]{:S(2)}, u32[]{:S(2)}) collective-permute-start(bf16[2,160,256]{2,1,0:T(8,128)(2,1)S(1)} %pad_maximum_fusion.1.x), channel_id=1, source_target_pairs={{16,32},{17,33},{18,34},{19,35},{20,36},{21,37},{22,38},{23,39},{2... | collective-permute-start | bytes 491528 | tf_op jit(solution)/shard_map/ppermute | solution.py:200
  8.0 1.9 %collective-permute-start = (bf16[2,160,256]{2,1,0:T(8,128)(2,1)S(1)}, bf16[2,160,256]{2,1,0:T(8,128)(2,1)S(1)}, u32[]{:S(2)}, u32[]{:S(2)}) collective-permute-start(bf16[2,160,256]{2,1,0:T(8,128)(2,1)S(1)} %pad_maximum_fusion.1.x), channel_id=1, source_target_pairs={{0,16},{1,17},{2,18},{3,19},{4,20},{5,21},{6,22},{7,23},{8,24},{9,... | collective-permute-start | bytes 491528 | tf_op jit(solution)/shard_map/ppermute | solution.py:200
  9.9 4.2 %collective-permute-done.1.xf = bf16[2,160,256]{2,1,0:T(8,128)(2,1)S(1)} collective-permute-done((bf16[2,160,256]{2,1,0:T(8,128)(2,1)S(1)}, bf16[2,160,256]{2,1,0:T(8,128)(2,1)S(1)}, u32[]{:S(2)}, u32[]{:S(2)}) %collective-permute-start.1) | collective-permute-done | bytes 163872 | tf_op jit(solution)/shard_map/ppermute | solution.py:200
  14.2 0.5 collective-permute-done.xe
  14.7 0.0 copy-done.3
  14.7 0.0 copy-done.4
  14.7 0.1 pad_maximum_fusion
  14.7 3.8 %collective-permute-start.5 = (bf16[6,160,256]{2,1,0:T(8,128)(2,1)S(1)}, bf16[6,160,256]{2,1,0:T(8,128)(2,1)S(1)}, u32[]{:S(2)}, u32[]{:S(2)}) collective-permute-start(bf16[6,160,256]{2,1,0:T(8,128)(2,1)S(1)} %pad_maximum_fusion), channel_id=1, source_target_pairs={{0,1},{1,0},{2,3},{3,2},{4,5},{5,4},{6,7},{7,6},{8,9},{9,8},{10,11... | collective-permute-start | bytes 1474568 | tf_op jit(solution)/shard_map/ppermute | solution.py:200
  18.5 3.8 %collective-permute-start.2 = (bf16[2,160,256]{2,1,0:T(8,128)(2,1)S(1)}, bf16[2,160,256]{2,1,0:T(8,128)(2,1)S(1)}, u32[]{:S(2)}, u32[]{:S(2)}) collective-permute-start(bf16[2,160,256]{2,1,0:T(8,128)(2,1)S(1)} %pad_maximum_fusion.1.x), channel_id=1, source_target_pairs={{1,2},{2,1},{3,4},{4,3},{5,6},{6,5},{7,8},{8,7},{9,10},{10,9},{11,... | collective-permute-start | bytes 491528 | tf_op jit(solution)/shard_map/ppermute | solution.py:200
  22.3 4.8 %collective-permute-done.2.xo = bf16[2,160,256]{2,1,0:T(8,128)(2,1)S(1)} collective-permute-done((bf16[2,160,256]{2,1,0:T(8,128)(2,1)S(1)}, bf16[2,160,256]{2,1,0:T(8,128)(2,1)S(1)}, u32[]{:S(2)}, u32[]{:S(2)}) %collective-permute-start.2) | collective-permute-done | bytes 163872 | tf_op jit(solution)/shard_map/ppermute | solution.py:200
  27.2 7.7 %collective-permute-start.4 = (bf16[2,160,256]{2,1,0:T(8,128)(2,1)S(1)}, bf16[2,160,256]{2,1,0:T(8,128)(2,1)S(1)}, u32[]{:S(2)}, u32[]{:S(2)}) collective-permute-start(bf16[2,160,256]{2,1,0:T(8,128)(2,1)S(1)} %collective-permute-done.2.xo), channel_id=1, source_target_pairs={{16,32},{17,33},{18,34},{19,35},{20,36},{21,37},{22,38},{23,39},{2... | collective-permute-start | bytes 491528 | tf_op jit(solution)/shard_map/ppermute | solution.py:200
  34.9 1.9 %collective-permute-start.3 = (bf16[2,160,256]{2,1,0:T(8,128)(2,1)S(1)}, bf16[2,160,256]{2,1,0:T(8,128)(2,1)S(1)}, u32[]{:S(2)}, u32[]{:S(2)}) collective-permute-start(bf16[2,160,256]{2,1,0:T(8,128)(2,1)S(1)} %collective-permute-done.2.xo), channel_id=1, source_target_pairs={{0,16},{1,17},{2,18},{3,19},{4,20},{5,21},{6,22},{7,23},{8,24},{9,... | collective-permute-start | bytes 491528 | tf_op jit(solution)/shard_map/ppermute | solution.py:200
  36.8 2.9 %collective-permute-done.4.xfo = bf16[2,160,256]{2,1,0:T(8,128)(2,1)S(1)} collective-permute-done((bf16[2,160,256]{2,1,0:T(8,128)(2,1)S(1)}, bf16[2,160,256]{2,1,0:T(8,128)(2,1)S(1)}, u32[]{:S(2)}, u32[]{:S(2)}) %collective-permute-start.4) | collective-permute-done | bytes 163872 | tf_op jit(solution)/shard_map/ppermute | solution.py:200
  39.8 2.1 %collective-permute-done.3.xeo = bf16[2,160,256]{2,1,0:T(8,128)(2,1)S(1)} collective-permute-done((bf16[2,160,256]{2,1,0:T(8,128)(2,1)S(1)}, bf16[2,160,256]{2,1,0:T(8,128)(2,1)S(1)}, u32[]{:S(2)}, u32[]{:S(2)}) %collective-permute-start.3) | collective-permute-done | bytes 163872 | tf_op jit(solution)/shard_map/ppermute | solution.py:200
  41.8 0.0 collective-permute-done.5.xp
  41.8 0.0 copy-start.2
  41.8 0.0 copy-done
  41.8 0.0 copy-done.1
  41.9 0.7 copy-done.2
  42.5 3.3 %attention.1 = (bf16[160,256]{1,0:T(8,128)(2,1)}, bf16[160,256]{1,0:T(8,128)(2,1)}, bf16[6,160,256]{2,1,0:T(8,128)(2,1)S(1)}, bf16[2,160,256]{2,1,0:T(8,128)(2,1...) custom-call(s32[1,1,2,2]{3,2,1,0:T(2,128)S(1)} %copy-done.2, ...), custom_call_target="tpu_custom_call" | custom-call | flops 262144000 | bytes 4194304 | tf_op jit(solution)/shard_map/attention/pallas_call | solution.py:155
  45.8 3.5 %collective-permute-start.6 = (bf16[6,160,256]{2,1,0:T(8,128)(2,1)S(1)}, bf16[6,160,256]{2,1,0:T(8,128)(2,1)S(1)}, u32[]{:S(2)}, u32[]{:S(2)}) collective-permute-start(bf16[6,160,256]{2,1,0:T(8,128)(2,1)S(1)} %get-tuple-element.16), channel_id=1, source_target_pairs={{0,1},{1,0},{2,3},{3,2},{4,5},{5,4},{6,7},{7,6},{8,9},{9,8},{10,11... | collective-permute-start | bytes 1474568 | tf_op jit(solution)/shard_map/ppermute | solution.py:200
  49.3 6.6 %collective-permute-start.9 = (bf16[2,160,256]{2,1,0:T(8,128)(2,1)S(1)}, bf16[2,160,256]{2,1,0:T(8,128)(2,1)S(1)}, u32[]{:S(2)}, u32[]{:S(2)}) collective-permute-start(bf16[2,160,256]{2,1,0:T(8,128)(2,1)S(1)} %get-tuple-element.20), channel_id=1, source_target_pairs={{16,32},{17,33},{18,34},{19,35},{20,36},{21,37},{22,38},{23,39},{2... | collective-permute-start | bytes 491528 | tf_op jit(solution)/shard_map/ppermute | solution.py:200
  55.9 1.9 %collective-permute-start.10 = (bf16[2,160,256]{2,1,0:T(8,128)(2,1)S(1)}, bf16[2,160,256]{2,1,0:T(8,128)(2,1)S(1)}, u32[]{:S(2)}, u32[]{:S(2)}) collective-permute-start(bf16[2,160,256]{2,1,0:T(8,128)(2,1)S(1)} %get-tuple-element.21), channel_id=1, source_target_pairs={{0,16},{1,17},{2,18},{3,19},{4,20},{5,21},{6,22},{7,23},{8,24},{9,... | collective-permute-start | bytes 491528 | tf_op jit(solution)/shard_map/ppermute | solution.py:200
  57.8 5.7 %collective-permute-done.9 = bf16[2,160,256]{2,1,0:T(8,128)(2,1)S(1)} collective-permute-done((bf16[2,160,256]{2,1,0:T(8,128)(2,1)S(1)}, bf16[2,160,256]{2,1,0:T(8,128)(2,1)S(1)}, u32[]{:S(2)}, u32[]{:S(2)}) %collective-permute-start.9) | collective-permute-done | bytes 163872 | tf_op jit(solution)/shard_map/ppermute | solution.py:200
  63.6 0.0 collective-permute-done.10
  63.6 0.1 add_convert_fusion
  63.6 4.0 %collective-permute-start.11 = (bf16[2,160,256]{2,1,0:T(8,128)(2,1)S(1)}, bf16[2,160,256]{2,1,0:T(8,128)(2,1)S(1)}, u32[]{:S(2)}, u32[]{:S(2)}) collective-permute-start(bf16[2,160,256]{2,1,0:T(8,128)(2,1)S(1)} %add_convert_fusion), channel_id=1, source_target_pairs={{1,2},{2,1},{3,4},{4,3},{5,6},{6,5},{7,8},{8,7},{9,10},{10,9},{11,... | collective-permute-start | bytes 491528 | tf_op jit(solution)/shard_map/ppermute | solution.py:200
  67.7 0.0 collective-permute-done.6
  67.7 0.1 convert_element_type.30
  67.8 0.1 fusion.1
  67.9 4.9 %collective-permute-start.7 = (bf16[2,160,256]{2,1,0:T(8,128)(2,1)S(1)}, bf16[2,160,256]{2,1,0:T(8,128)(2,1)S(1)}, u32[]{:S(2)}, u32[]{:S(2)}) collective-permute-start(bf16[2,160,256]{2,1,0:T(8,128)(2,1)S(1)} %get-tuple-element.22), channel_id=1, source_target_pairs={{16,32},{17,33},{18,34},{19,35},{20,36},{21,37},{22,38},{23,39},{2... | collective-permute-start | bytes 491528 | tf_op jit(solution)/shard_map/ppermute | solution.py:200
  72.8 1.9 %collective-permute-start.8 = (bf16[2,160,256]{2,1,0:T(8,128)(2,1)S(1)}, bf16[2,160,256]{2,1,0:T(8,128)(2,1)S(1)}, u32[]{:S(2)}, u32[]{:S(2)}) collective-permute-start(bf16[2,160,256]{2,1,0:T(8,128)(2,1)S(1)} %get-tuple-element.23), channel_id=1, source_target_pairs={{0,16},{1,17},{2,18},{3,19},{4,20},{5,21},{6,22},{7,23},{8,24},{9,... | collective-permute-start | bytes 491528 | tf_op jit(solution)/shard_map/ppermute | solution.py:200
  74.7 1.3 %collective-permute-done.11 = bf16[2,160,256]{2,1,0:T(8,128)(2,1)S(1)} collective-permute-done((bf16[2,160,256]{2,1,0:T(8,128)(2,1)S(1)}, bf16[2,160,256]{2,1,0:T(8,128)(2,1)S(1)}, u32[]{:S(2)}, u32[]{:S(2)}) %collective-permute-start.11) | collective-permute-done | bytes 163872 | tf_op jit(solution)/shard_map/ppermute | solution.py:200
  76.0 6.5 %collective-permute-done.7 = bf16[2,160,256]{2,1,0:T(8,128)(2,1)S(1)} collective-permute-done((bf16[2,160,256]{2,1,0:T(8,128)(2,1)S(1)}, bf16[2,160,256]{2,1,0:T(8,128)(2,1)S(1)}, u32[]{:S(2)}, u32[]{:S(2)}) %collective-permute-start.7) | collective-permute-done | bytes 163872 | tf_op jit(solution)/shard_map/ppermute | solution.py:200
  82.5 0.0 collective-permute-done.8
  82.5 0.1 fusion.5
  82.6 0.7 fusion.6
Async XLA Ops:
  0.6 14.0 %copy-start.3 = (bf16[1,2,80,256]{3,2,1,0:T(8,128)(2,1)S(1)}, bf16[1,2,80,256]{3,2,1,0:T(8,128)(2,1)}, u32[]{:S(2)}) copy-start(bf16[1,2,80,256]{3,2,1,0:T(8,128)(2,1)} %param.7) | copy-start | bytes 245764
  0.6 14.0 %copy-start.4 = (bf16[1,2,80,256]{3,2,1,0:T(8,128)(2,1)S(1)}, bf16[1,2,80,256]{3,2,1,0:T(8,128)(2,1)}, u32[]{:S(2)}) copy-start(bf16[1,2,80,256]{3,2,1,0:T(8,128)(2,1)} %param.6) | copy-start | bytes 245764
  1.6 40.2 %copy-start = (bf16[1,2,80,256]{3,2,1,0:T(8,128)(2,1)S(1)}, bf16[1,2,80,256]{3,2,1,0:T(8,128)(2,1)}, u32[]{:S(2)}) copy-start(bf16[1,2,80,256]{3,2,1,0:T(8,128)(2,1)} %param.5) | copy-start | bytes 245764
  1.6 40.2 %copy-start.1 = (bf16[1,2,80,256]{3,2,1,0:T(8,128)(2,1)S(1)}, bf16[1,2,80,256]{3,2,1,0:T(8,128)(2,1)}, u32[]{:S(2)}) copy-start(bf16[1,2,80,256]{3,2,1,0:T(8,128)(2,1)} %param.8) | copy-start | bytes 245764
  1.7 12.5 %collective-permute-start.1 = (bf16[2,160,256]{2,1,0:T(8,128)(2,1)S(1)}, bf16[2,160,256]{2,1,0:T(8,128)(2,1)S(1)}, u32[]{:S(2)}, u32[]{:S(2)}) collective-permute-start(bf16[2,160,256]{2,1,0:T(8,128)(2,1)S(1)} %pad_maximum_fusion.1.x), channel_id=1, source_target_pairs={{16,32},{17,33},{18,34},{19,35},{20,36},{21,37},{22,38},{23,39},{2... | collective-permute-start | bytes 491528 | tf_op jit(solution)/shard_map/ppermute | solution.py:200
  8.0 6.6 %collective-permute-start = (bf16[2,160,256]{2,1,0:T(8,128)(2,1)S(1)}, bf16[2,160,256]{2,1,0:T(8,128)(2,1)S(1)}, u32[]{:S(2)}, u32[]{:S(2)}) collective-permute-start(bf16[2,160,256]{2,1,0:T(8,128)(2,1)S(1)} %pad_maximum_fusion.1.x), channel_id=1, source_target_pairs={{0,16},{1,17},{2,18},{3,19},{4,20},{5,21},{6,22},{7,23},{8,24},{9,... | collective-permute-start | bytes 491528 | tf_op jit(solution)/shard_map/ppermute | solution.py:200
  14.7 27.1 %collective-permute-start.5 = (bf16[6,160,256]{2,1,0:T(8,128)(2,1)S(1)}, bf16[6,160,256]{2,1,0:T(8,128)(2,1)S(1)}, u32[]{:S(2)}, u32[]{:S(2)}) collective-permute-start(bf16[6,160,256]{2,1,0:T(8,128)(2,1)S(1)} %pad_maximum_fusion), channel_id=1, source_target_pairs={{0,1},{1,0},{2,3},{3,2},{4,5},{5,4},{6,7},{7,6},{8,9},{9,8},{10,11... | collective-permute-start | bytes 1474568 | tf_op jit(solution)/shard_map/ppermute | solution.py:200
  18.5 8.7 %collective-permute-start.2 = (bf16[2,160,256]{2,1,0:T(8,128)(2,1)S(1)}, bf16[2,160,256]{2,1,0:T(8,128)(2,1)S(1)}, u32[]{:S(2)}, u32[]{:S(2)}) collective-permute-start(bf16[2,160,256]{2,1,0:T(8,128)(2,1)S(1)} %pad_maximum_fusion.1.x), channel_id=1, source_target_pairs={{1,2},{2,1},{3,4},{4,3},{5,6},{6,5},{7,8},{8,7},{9,10},{10,9},{11,... | collective-permute-start | bytes 491528 | tf_op jit(solution)/shard_map/ppermute | solution.py:200
  27.2 12.6 %collective-permute-start.4 = (bf16[2,160,256]{2,1,0:T(8,128)(2,1)S(1)}, bf16[2,160,256]{2,1,0:T(8,128)(2,1)S(1)}, u32[]{:S(2)}, u32[]{:S(2)}) collective-permute-start(bf16[2,160,256]{2,1,0:T(8,128)(2,1)S(1)} %collective-permute-done.2.xo), channel_id=1, source_target_pairs={{16,32},{17,33},{18,34},{19,35},{20,36},{21,37},{22,38},{23,39},{2... | collective-permute-start | bytes 491528 | tf_op jit(solution)/shard_map/ppermute | solution.py:200
  34.9 6.9 %collective-permute-start.3 = (bf16[2,160,256]{2,1,0:T(8,128)(2,1)S(1)}, bf16[2,160,256]{2,1,0:T(8,128)(2,1)S(1)}, u32[]{:S(2)}, u32[]{:S(2)}) collective-permute-start(bf16[2,160,256]{2,1,0:T(8,128)(2,1)S(1)} %collective-permute-done.2.xo), channel_id=1, source_target_pairs={{0,16},{1,17},{2,18},{3,19},{4,20},{5,21},{6,22},{7,23},{8,24},{9,... | collective-permute-start | bytes 491528 | tf_op jit(solution)/shard_map/ppermute | solution.py:200
  41.8 0.7 copy-start.2
  45.8 21.9 %collective-permute-start.6 = (bf16[6,160,256]{2,1,0:T(8,128)(2,1)S(1)}, bf16[6,160,256]{2,1,0:T(8,128)(2,1)S(1)}, u32[]{:S(2)}, u32[]{:S(2)}) collective-permute-start(bf16[6,160,256]{2,1,0:T(8,128)(2,1)S(1)} %get-tuple-element.16), channel_id=1, source_target_pairs={{0,1},{1,0},{2,3},{3,2},{4,5},{5,4},{6,7},{7,6},{8,9},{9,8},{10,11... | collective-permute-start | bytes 1474568 | tf_op jit(solution)/shard_map/ppermute | solution.py:200
  49.3 14.3 %collective-permute-start.9 = (bf16[2,160,256]{2,1,0:T(8,128)(2,1)S(1)}, bf16[2,160,256]{2,1,0:T(8,128)(2,1)S(1)}, u32[]{:S(2)}, u32[]{:S(2)}) collective-permute-start(bf16[2,160,256]{2,1,0:T(8,128)(2,1)S(1)} %get-tuple-element.20), channel_id=1, source_target_pairs={{16,32},{17,33},{18,34},{19,35},{20,36},{21,37},{22,38},{23,39},{2... | collective-permute-start | bytes 491528 | tf_op jit(solution)/shard_map/ppermute | solution.py:200
  55.9 7.6 %collective-permute-start.10 = (bf16[2,160,256]{2,1,0:T(8,128)(2,1)S(1)}, bf16[2,160,256]{2,1,0:T(8,128)(2,1)S(1)}, u32[]{:S(2)}, u32[]{:S(2)}) collective-permute-start(bf16[2,160,256]{2,1,0:T(8,128)(2,1)S(1)} %get-tuple-element.21), channel_id=1, source_target_pairs={{0,16},{1,17},{2,18},{3,19},{4,20},{5,21},{6,22},{7,23},{8,24},{9,... | collective-permute-start | bytes 491528 | tf_op jit(solution)/shard_map/ppermute | solution.py:200
  63.6 12.4 %collective-permute-start.11 = (bf16[2,160,256]{2,1,0:T(8,128)(2,1)S(1)}, bf16[2,160,256]{2,1,0:T(8,128)(2,1)S(1)}, u32[]{:S(2)}, u32[]{:S(2)}) collective-permute-start(bf16[2,160,256]{2,1,0:T(8,128)(2,1)S(1)} %add_convert_fusion), channel_id=1, source_target_pairs={{1,2},{2,1},{3,4},{4,3},{5,6},{6,5},{7,8},{8,7},{9,10},{10,9},{11,... | collective-permute-start | bytes 491528 | tf_op jit(solution)/shard_map/ppermute | solution.py:200
  67.9 14.6 %collective-permute-start.7 = (bf16[2,160,256]{2,1,0:T(8,128)(2,1)S(1)}, bf16[2,160,256]{2,1,0:T(8,128)(2,1)S(1)}, u32[]{:S(2)}, u32[]{:S(2)}) collective-permute-start(bf16[2,160,256]{2,1,0:T(8,128)(2,1)S(1)} %get-tuple-element.22), channel_id=1, source_target_pairs={{16,32},{17,33},{18,34},{19,35},{20,36},{21,37},{22,38},{23,39},{2... | collective-permute-start | bytes 491528 | tf_op jit(solution)/shard_map/ppermute | solution.py:200
  72.8 9.7 %collective-permute-start.8 = (bf16[2,160,256]{2,1,0:T(8,128)(2,1)S(1)}, bf16[2,160,256]{2,1,0:T(8,128)(2,1)S(1)}, u32[]{:S(2)}, u32[]{:S(2)}) collective-permute-start(bf16[2,160,256]{2,1,0:T(8,128)(2,1)S(1)} %get-tuple-element.23), channel_id=1, source_target_pairs={{0,16},{1,17},{2,18},{3,19},{4,20},{5,21},{6,22},{7,23},{8,24},{9,... | collective-permute-start | bytes 491528 | tf_op jit(solution)/shard_map/ppermute | solution.py:200

commit v2 on v1

v2 whole, which is shorter than its diff:
```python
import functools

import jax
import jax.numpy as jnp
from jax import lax
from jax.experimental import pallas as pl
from jax.experimental.pallas import tpu as pltpu
from jax.sharding import PartitionSpec as P

W = 80
WT = 8
GROUPS = W // WT
TOK = 160
HEADS = 2
HD = 128
CHANS = HEADS * HD
BLOCKS = W // 16
TILE = 256
SLOTS = 8
BLOCK = 2 * SLOTS * 16
NEG = -1e30
LOG2E = 1.4426950408889634
SCALE = HD ** (-0.5)
BOTH = ("frame", "height")
F32, BF16 = jnp.float32, jnp.bfloat16


def near(j):
    second = slice(max(2 * j - 1, 0) * 16, (2 * j + 1) * 16)
    first = slice((2 * j + 1) * 16, min(2 * j + 3, GROUPS) * 16)
    return second, first


def dot_nt(a, b):
    return lax.dot_general(a, b, (((1,), (1,)), ((), ())), preferred_element_type=jnp.float32)


def dot_nn(a, b):
    return lax.dot_general(a, b, (((1,), (0,)), ((), ())), preferred_element_type=jnp.float32)


def dot_tn(a, b):
    return lax.dot_general(a, b, (((0,), (0,)), ((), ())), preferred_element_type=jnp.float32)


def by_group(ref):
    wide = ref[...].astype(jnp.float32)
    parts = []
    for g in range(GROUPS):
        for r in range(2):
            parts.append(wide[r * W + g * WT : r * W + (g + 1) * WT])
    return jnp.concatenate(parts, axis=0).astype(jnp.bfloat16)


def by_row(wide):
    parts = []
    for r in range(2):
        for g in range(GROUPS):
            parts.append(wide[g * 16 + r * WT : g * 16 + (r + 1) * WT])
    return jnp.concatenate(parts, axis=0).astype(jnp.bfloat16)


def prepare_kernel(nframe, nheight, reach, q, o, qs, os_, bias):
    qs[...] = by_group(q)
    os_[...] = by_group(o)
    frame, height = lax.axis_index("frame"), lax.axis_index("height")
    fo_ok = (frame > 0) & (frame < nframe - 1)
    o_ok = (height > 0) & (height < nheight - 1)
    slot = lax.broadcasted_iota(jnp.int32, (8, BLOCK), 1) // 32
    at_p = (slot == 1) | (slot == 4) | (slot == 7)
    at_o = (slot == 2) | (slot == 5)
    at_fe = (slot >= 3) & (slot <= 5)
    at_fo = slot >= 6
    corner_row = lax.broadcasted_iota(jnp.int32, (8, BLOCK), 0) == 1
    zero, neg = jnp.float32(0), jnp.float32(NEG)
    for h in range(HEADS):
        frames = reach[0, 0, h, 0] > 0
        rows = reach[0, 0, h, 1] > 0
        fe_b = jnp.where(frames, zero, neg)
        fo_b = jnp.where(frames & fo_ok, zero, neg)
        p_b = jnp.where(rows, zero, neg)
        o_b = jnp.where(rows & o_ok, zero, neg)
        ok = jnp.where(at_fe, fe_b, jnp.where(at_fo, fo_b, zero))
        ok = jnp.minimum(ok, jnp.where(at_p, p_b, jnp.where(at_o, o_b, zero)))
        bias[h] = jnp.where(corner_row, jnp.minimum(fo_b, o_b), ok)


def softmax_kernel(
    qs, os_, bias, x, xf, xe, xo, xfo, xeo, xp,
    gfo_, pm, gm, pc, gc, ks, vs, kc, vc,
    sm, dm, sc, dc,
):
    height = lax.axis_index("height")
    xp = xp.at[1 - lax.rem(height, 2)]
    slots = [(x, 0), (xp, 0), (xo, 0), (xe, 0), (xp, 4), (xeo, 0), (xf, 0), (xp, 2)]
    for j in range(BLOCKS):
        for r in range(2):
            src = slice(r * W + 16 * j, r * W + 16 * j + 16)
            for slot, (ref, at) in enumerate(slots):
                row = j * BLOCK + (slot * 2 + r) * 16
                ks[row : row + 16] = ref[at, src]
                vs[row : row + 16] = ref[at + 1, src]
            row = j * 32 + r * 16
            kc[row : row + 16] = xfo[0, src]
            vc[row : row + 16] = xfo[1, src]
    kc[TOK:] = jnp.zeros((TILE - TOK, CHANS), BF16)
    vc[TOK:] = jnp.zeros((TILE - TOK, CHANS), BF16)

    lane = lax.broadcasted_iota(jnp.int32, (1, BLOCK), 1)
    half = (lane % 16) // WT
    corner_group = jnp.where(lane < TOK, (lane // 32) * 2 + half, 1000)

    for h in range(HEADS):
        hs = slice(h * HD, (h + 1) * HD)
        for j in range(BLOCKS):
            kr = slice(j * BLOCK, (j + 1) * BLOCK)
            second, first = near(j)
            both = slice(second.start, first.stop)
            cut = second.stop - second.start
            for left, right, out in ((qs, ks, sm), (os_, vs, dm)):
                t = dot_nt(left[both, hs], right[kr, hs])
                out[second, BLOCK:] = t[:cut]
                out[first, :BLOCK] = t[cut:]
        sc[...] = dot_nt(qs[:, hs], kc[:, hs])
        dc[...] = dot_nt(os_[:, hs], vc[:, hs])
        ok, corner_ok = bias[h, 0:1], bias[h, 1:2]
        only_last = jnp.where(half == 1, ok, NEG)
        only_first = jnp.where(half == 0, ok, NEG)
        for g in range(GROUPS):
            qr = slice(g * 16, (g + 1) * 16)
            halves = [(slice(0, BLOCK), only_last if g % 2 == 0 else ok)] if g > 0 else []
            if g < GROUPS - 1:
                halves.append((slice(BLOCK, 2 * BLOCK), ok if g % 2 == 0 else only_first))
            corner = jnp.where(jnp.abs(corner_group - g) <= 1, corner_ok, NEG)
            s = [sm[qr, kr] * (SCALE * LOG2E) + add for kr, add in halves]
            s.append(sc[qr] * (SCALE * LOG2E) + corner)
            d = [dm[qr, kr] for kr, _ in halves] + [dc[qr]]
            top = functools.reduce(jnp.maximum, s)
            top = jnp.max(top, axis=1, keepdims=True)
            e = [jnp.exp2(v - top) for v in s]
            inv = 1.0 / jnp.sum(sum(e[1:], e[0]), axis=1, keepdims=True)
            p = [v * inv for v in e]
            pd = [a * b for a, b in zip(p, d)]
            delta = jnp.sum(sum(pd[1:], pd[0]), axis=1, keepdims=True)
            g_s = [((a * (b - delta)) * SCALE).astype(BF16) for a, b in zip(p, d)]
            for (kr, _), a, b in zip(halves, p, g_s):
                pm[h, qr, kr] = a.astype(BF16)
                gm[h, qr, kr] = b
            pc[h, qr] = p[-1].astype(BF16)
            gc[h, qr] = g_s[-1]
        for at, left, right in ((0, gc, qs), (1, pc, os_)):
            t = dot_tn(left[h], right[:, hs]).astype(BF16)
            for j in range(BLOCKS):
                for r in range(2):
                    dst = slice(r * W + 16 * j, r * W + 16 * j + 16)
                    row = j * 32 + r * 16
                    gfo_[at, dst, hs] = t[row : row + 16]


def key_kernel(qs, os_, pm, gm, ge, geo, go, gfe, gfo, gown):
    outs = [(gown, 0), (ge, 0), (go, 0), (gfe, 0), (ge, 2), (geo, 0), (gfo, 0), (ge, 4)]
    for h in range(HEADS):
        hs = slice(h * HD, (h + 1) * HD)
        for j in range(BLOCKS):
            second, first = near(j)
            both = slice(second.start, first.stop)
            for add, left, right in ((0, gm, qs), (1, pm, os_)):
                t = jnp.concatenate([left[h, second, BLOCK:], left[h, first, :BLOCK]], axis=0)
                t = dot_tn(t, right[both, hs])
                for slot, (ref, at) in enumerate(outs):
                    for r in range(2):
                        dst = slice(r * W + 16 * j, r * W + 16 * j + 16)
                        row = (slot * 2 + r) * 16
                        ref[at + add, dst, hs] = t[row : row + 16].astype(ref.dtype)


def query_kernel(ks, vs, kc, vc, pm, gm, pc, gc, att, gq):
    for h in range(HEADS):
        hs = slice(h * HD, (h + 1) * HD)
        for main, corner, right, right_c, out in ((pm, pc, vs, vc, att), (gm, gc, ks, kc, gq)):
            parts = [dot_nn(main[h, :16, BLOCK:], right[:BLOCK, hs])]
            for j in range(1, BLOCKS):
                qr = slice((2 * j - 1) * 16, (2 * j + 1) * 16)
                parts.append(dot_nn(main[h, qr], right[(j - 1) * BLOCK : (j + 1) * BLOCK, hs]))
            parts.append(dot_nn(main[h, TOK - 16 :, :BLOCK], right[(BLOCKS - 1) * BLOCK :, hs]))
            t = jnp.concatenate(parts, axis=0) + dot_nn(corner[h], right_c[:, hs])
            out[:, hs] = by_row(t)


def call(body, name, flops, ins, outs, scratch=(), smem=0):
    vmem = pl.BlockSpec(memory_space=pltpu.VMEM)
    return pl.pallas_call(
        body,
        out_shape=tuple(jax.ShapeDtypeStruct(shape, kind) for shape, kind in outs),
        in_specs=[pl.BlockSpec(memory_space=pltpu.SMEM)] * smem + [vmem] * (len(ins) - smem),
        out_specs=(vmem,) * len(outs),
        scratch_shapes=[pltpu.VMEM(shape, kind) for shape, kind in scratch],
        compiler_params=pltpu.CompilerParams(vmem_limit_bytes=32 * 1024 * 1024),
        cost_estimate=pl.CostEstimate(flops=flops, bytes_accessed=2 * 1024 * 1024, transcendentals=0),
        name=name,
    )(*ins)


def swaps():
    nf, nh = lax.axis_size("frame"), lax.axis_size("height")
    even = lambda i: i ^ 1
    odd = lambda i: ((i + 1) ^ 1) - 1
    along_f = lambda to: [
        (f * nh + h, to(f) * nh + h) for f in range(nf) for h in range(nh) if 0 <= to(f) < nf
    ]
    along_h = lambda to: [
        (f * nh + h, f * nh + to(h)) for f in range(nf) for h in range(nh) if 0 <= to(h) < nh
    ]
    return along_f(even), along_f(odd), along_h(even), along_h(odd)


def local(queries, keys, values, d_out, reach):
    fe, fo, he, ho = swaps()
    swap = lambda array, pairs: lax.ppermute(array, BOTH, pairs)
    chip = [list(pair) for pair in he if pair[0] < pair[1]]
    share = lambda v: lax.all_gather(v, BOTH, axis_index_groups=chip)
    nframe, nheight = lax.axis_size("frame"), lax.axis_size("height")
    shape = queries.shape
    tile, pair = (TOK, CHANS), (2, TOK, CHANS)
    q, o = queries.reshape(tile), d_out.reshape(tile)
    x = jnp.stack([keys.reshape(tile), values.reshape(tile)])
    xf = swap(x, fo)
    xo = swap(x, ho)
    xe = swap(x, fe)
    xfo = swap(xo, fo)
    xeo = swap(xo, fe)
    xp = share(jnp.concatenate([x, xf, xe]))
    keys_all, keys_corner = (BLOCKS * BLOCK, CHANS), (TILE, CHANS)
    main, corner = (HEADS, TOK, 2 * BLOCK), (HEADS, TOK, TILE)
    qs, os_, bias = call(
        functools.partial(prepare_kernel, nframe, nheight), "prepare", 10**8, (reach, q, o),
        [(tile, BF16)] * 2 + [((HEADS, 8, BLOCK), F32)], (), 1,
    )
    gfo_, pm, gm, pc, gc, ks, vs, kc, vc = call(
        softmax_kernel, "softmax", 2 * 10**9, (qs, os_, bias, x, xf, xe, xo, xfo, xeo, xp),
        [(pair, BF16)] + [(main, BF16)] * 2 + [(corner, BF16)] * 2
        + [(keys_all, BF16)] * 2 + [(keys_corner, BF16)] * 2,
        [((TOK, 2 * BLOCK), F32)] * 2 + [((TOK, TILE), F32)] * 2,
    )
    ge, geo, go, gfe, gfo, gown = call(
        key_kernel, "keys", 10**9, (qs, os_, pm, gm),
        [((6, TOK, CHANS), BF16), (pair, BF16)] + [(pair, F32)] * 4,
    )
    att, gq = call(
        query_kernel, "queries", 10**9, (ks, vs, kc, vc, pm, gm, pc, gc), [(tile, BF16)] * 2
    )
    other = 1 - lax.axis_index("height") % 2
    rp = lax.dynamic_index_in_dim(share(ge), other, 0, False).astype(F32)
    rco = swap(gfo_, ho).astype(F32)
    reo = swap(geo, fe).astype(F32)
    to_fo = (gfo + rp[4:6] + rco).astype(BF16)
    to_fo, gfe, go = lax.optimization_barrier((to_fo, gfe, go))
    rf = swap(to_fo, fo).astype(F32)
    re = swap((gfe + rp[2:4]).astype(BF16), fe).astype(F32)
    ro = swap((go + reo).astype(BF16), ho).astype(F32)
    total = (gown + rp[0:2] + ro + re + rf).astype(BF16)
    return (
        att.reshape(shape), gq.reshape(shape), total[0].reshape(shape), total[1].reshape(shape)
    )


def solution(mesh):
    spec = P("frame", "height", None, None)
    return jax.shard_map(
        local, mesh=mesh, in_specs=(spec,) * 5, out_specs=(spec,) * 4, check_vma=False
    )
```

time: 83.7 us -> 58.9 us (0.70)
  the two profiles are of different devices: /device:TPU:189 before, /device:TPU:321 now
where the time goes in v2:
time: 58.9 us; the launch traced here: 58.5 us
  starting transfers between devices  34.6 us (59%)
  waiting for transfers between devices  10.5 us (18%)
  blocking collectives  5.79 us (10%)
  Pallas kernels  4.03 us (7%)
  other arithmetic  1.36 us (2%)
  local copies, waits for them, and re-layouts  1.34 us (2%)
  between operations  0.89 us (2%)
    ppermute x10, starting transfers between devices, local(): swap = lambda array, pairs: lax.ppermute(array, BOTH, pairs)  34.6 us
    ppermute x10, waiting for transfers between devices, local(): swap = lambda array, pairs: lax.ppermute(array, BOTH, pairs)  10.5 us
    all_gather x2, blocking collectives, local(): share = lambda v: lax.all_gather(v, BOTH, axis_index_groups=chip)  5.79 us
    pallas_call x4, Pallas kernels, call(): pl.pallas_call(body, out_shape=tuple((jax.ShapeDtypeStruct(shape, kind) f...  4.03 us
  transfers between devices with their start and end apart: 10, of which 3 were waited for; matrix products, arithmetic and copies ran while one was open for 0% of the time, Pallas kernels for 4%

profile of v2, /device:TPU:321, one launch (start us, length us, event | category | flops | bytes accessed | tf_op | source)
XLA Modules:
  0.0 58.5 jit_solution(7568094867408277114)
XLA Ops:
  0.6 0.0 copy-start
  0.6 0.0 copy-start.1
  0.7 1.0 %pad_maximum_fusion.1.x = bf16[2,160,256]{2,1,0:T(8,128)(2,1)S(1)} fusion(bf16[1,160,256]{2,1,0:T(8,128)(2,1)} %bitcast.40, bf16[1,160,256]{2,1,0:T(8,128)(2,1)} %bitcast.42), kind=kLoop, calls=%fused_computation.16 | loop fusion | flops 81920 | bytes 327680 | tf_op jit(solution)/shard_map/stack | solution.py:226
  1.6 3.7 %collective-permute-start.2 = (bf16[2,160,256]{2,1,0:T(8,128)(2,1)S(1)}, bf16[2,160,256]{2,1,0:T(8,128)(2,1)S(1)}, u32[]{:S(2)}, u32[]{:S(2)}) collective-permute-start(bf16[2,160,256]{2,1,0:T(8,128)(2,1)S(1)} %pad_maximum_fusion.1.x), channel_id=1, source_target_pairs={{1,2},{2,1},{3,4},{4,3},{5,6},{6,5},{7,8},{8,7},{9,10},{10,9},{11,... | collective-permute-start | bytes 491528 | tf_op jit(solution)/shard_map/ppermute | solution.py:219
  5.3 3.3 %collective-permute-start = (bf16[2,160,256]{2,1,0:T(8,128)(2,1)S(1)}, bf16[2,160,256]{2,1,0:T(8,128)(2,1)S(1)}, u32[]{:S(2)}, u32[]{:S(2)}) collective-permute-start(bf16[2,160,256]{2,1,0:T(8,128)(2,1)S(1)} %pad_maximum_fusion.1.x), channel_id=1, source_target_pairs={{16,32},{17,33},{18,34},{19,35},{20,36},{21,37},{22,38},{23,39},{2... | collective-permute-start | bytes 491528 | tf_op jit(solution)/shard_map/ppermute | solution.py:219
  8.6 3.1 %collective-permute-start.1 = (bf16[2,160,256]{2,1,0:T(8,128)(2,1)S(1)}, bf16[2,160,256]{2,1,0:T(8,128)(2,1)S(1)}, u32[]{:S(2)}, u32[]{:S(2)}) collective-permute-start(bf16[2,160,256]{2,1,0:T(8,128)(2,1)S(1)} %pad_maximum_fusion.1.x), channel_id=1, source_target_pairs={{0,16},{1,17},{2,18},{3,19},{4,20},{5,21},{6,22},{7,23},{8,24},{9,... | collective-permute-start | bytes 491528 | tf_op jit(solution)/shard_map/ppermute | solution.py:219
  11.8 0.0 copy-start.2
  11.8 0.0 copy-done
  11.8 0.0 copy-done.1
  11.8 0.7 %copy-done.2 = s32[1,1,2,2]{3,2,1,0:T(2,128)S(1)} copy-done((s32[1,1,2,2]{3,2,1,0:T(2,128)S(1)}, s32[1,1,2,2]{3,2,1,0:T(2,128)}, u32[]{:S(2)}) %copy-start.2) | copy-done | bytes 40
  12.4 0.0 copy-start.3
  12.4 0.0 copy-start.4
  12.4 0.6 prepare.1
  13.0 0.0 collective-permute-done.2.xo
  13.0 6.0 %collective-permute-start.3 = (bf16[2,160,256]{2,1,0:T(8,128)(2,1)S(1)}, bf16[2,160,256]{2,1,0:T(8,128)(2,1)S(1)}, u32[]{:S(2)}, u32[]{:S(2)}) collective-permute-start(bf16[2,160,256]{2,1,0:T(8,128)(2,1)S(1)} %collective-permute-done.2.xo), channel_id=1, source_target_pairs={{16,32},{17,33},{18,34},{19,35},{20,36},{21,37},{22,38},{23,39},{2... | collective-permute-start | bytes 491528 | tf_op jit(solution)/shard_map/ppermute | solution.py:219
  19.0 1.9 %collective-permute-start.4 = (bf16[2,160,256]{2,1,0:T(8,128)(2,1)S(1)}, bf16[2,160,256]{2,1,0:T(8,128)(2,1)S(1)}, u32[]{:S(2)}, u32[]{:S(2)}) collective-permute-start(bf16[2,160,256]{2,1,0:T(8,128)(2,1)S(1)} %collective-permute-done.2.xo), channel_id=1, source_target_pairs={{0,16},{1,17},{2,18},{3,19},{4,20},{5,21},{6,22},{7,23},{8,24},{9,... | collective-permute-start | bytes 491528 | tf_op jit(solution)/shard_map/ppermute | solution.py:219
  20.9 0.0 collective-permute-done.xf
  20.9 0.0 collective-permute-done.1.xe
  21.0 0.0 copy-done.3
  21.0 0.0 copy-done.4
  21.0 0.1 pad_maximum_fusion
  21.0 3.3 %all-gather = bf16[12,160,256]{2,1,0:T(8,128)(2,1)S(1)} all-gather(bf16[6,160,256]{2,1,0:T(8,128)(2,1)S(1)} %pad_maximum_fusion), channel_id=2, replica_groups={{0,1},{2,3},{4,5},{6,7},{8,9},{10,11},{12,13},{14,15},{16,17},{18,19},{..., dimensions={0}, use_global_device_ids=true | all-gather | bytes 1474560 | tf_op jit(solution)/shard_map/all_gather | solution.py:221
  24.3 3.6 %collective-permute-done.3.xfo = bf16[2,160,256]{2,1,0:T(8,128)(2,1)S(1)} collective-permute-done((bf16[2,160,256]{2,1,0:T(8,128)(2,1)S(1)}, bf16[2,160,256]{2,1,0:T(8,128)(2,1)S(1)}, u32[]{:S(2)}, u32[]{:S(2)}) %collective-permute-start.3) | collective-permute-done | bytes 163872 | tf_op jit(solution)/shard_map/ppermute | solution.py:219
  27.9 0.0 collective-permute-done.4.xeo
  27.9 1.7 %softmax.1 = (bf16[2,160,256]{2,1,0:T(8,128)(2,1)S(1)}, bf16[2,160,512]{2,1,0:T(8,128)(2,1)S(1)}, bf16[2,160,512]{2,1,0:T(8,128)(2,1)S(1)}, bf16[2,160,256]{2,1,...) custom-call(bf16[160,256]{1,0:T(8,128)(2,1)S(1)} %get-tuple-element., ...), custom_call_target="tpu_custom_call" | custom-call | flops 2000000000 | bytes 2097152 | tf_op jit(solution)/shard_map/softmax/pallas_call | solution.py:192
  29.6 4.5 %collective-permute-start.5 = (bf16[2,160,256]{2,1,0:T(8,128)(2,1)S(1)}, bf16[2,160,256]{2,1,0:T(8,128)(2,1)S(1)}, u32[]{:S(2)}, u32[]{:S(2)}) collective-permute-start(bf16[2,160,256]{2,1,0:T(8,128)(2,1)S(1)} %get-tuple-element.43), channel_id=1, source_target_pairs={{1,2},{2,1},{3,4},{4,3},{5,6},{6,5},{7,8},{8,7},{9,10},{10,9},{11,... | collective-permute-start | bytes 491528 | tf_op jit(solution)/shard_map/ppermute | solution.py:219
  34.1 0.6 keys.1
  34.7 2.5 %all-gather.1 = bf16[12,160,256]{2,1,0:T(8,128)(2,1)S(1)} all-gather(bf16[6,160,256]{2,1,0:T(8,128)(2,1)S(1)} %get-tuple-element.41), channel_id=3, replica_groups={{0,1},{2,3},{4,5},{6,7},{8,9},{10,11},{12,13},{14,15},{16,17},{18,19},{..., dimensions={0}, use_global_device_ids=true | all-gather | bytes 1474560 | tf_op jit(solution)/shard_map/all_gather | solution.py:221
  37.2 1.9 %collective-permute-start.6 = (bf16[2,160,256]{2,1,0:T(8,128)(2,1)S(1)}, bf16[2,160,256]{2,1,0:T(8,128)(2,1)S(1)}, u32[]{:S(2)}, u32[]{:S(2)}) collective-permute-start(bf16[2,160,256]{2,1,0:T(8,128)(2,1)S(1)} %get-tuple-element.47), channel_id=1, source_target_pairs={{0,16},{1,17},{2,18},{3,19},{4,20},{5,21},{6,22},{7,23},{8,24},{9,... | collective-permute-start | bytes 491528 | tf_op jit(solution)/shard_map/ppermute | solution.py:219
  39.1 0.1 dynamic-slice_convert_fusion
  39.2 0.0 collective-permute-done.5
  39.2 0.1 fusion.4
  39.3 5.1 %collective-permute-start.9 = (bf16[2,160,256]{2,1,0:T(8,128)(2,1)S(1)}, bf16[2,160,256]{2,1,0:T(8,128)(2,1)S(1)}, u32[]{:S(2)}, u32[]{:S(2)}) collective-permute-start(bf16[2,160,256]{2,1,0:T(8,128)(2,1)S(1)} %fusion.4), channel_id=1, source_target_pairs={{16,32},{17,33},{18,34},{19,35},{20,36},{21,37},{22,38},{23,39},{2... | collective-permute-start | bytes 491528 | tf_op jit(solution)/shard_map/ppermute | solution.py:219
  44.4 1.9 %collective-permute-start.8 = (bf16[2,160,256]{2,1,0:T(8,128)(2,1)S(1)}, bf16[2,160,256]{2,1,0:T(8,128)(2,1)S(1)}, u32[]{:S(2)}, u32[]{:S(2)}) collective-permute-start(bf16[2,160,256]{2,1,0:T(8,128)(2,1)S(1)} %fusion.1), channel_id=1, source_target_pairs={{0,16},{1,17},{2,18},{3,19},{4,20},{5,21},{6,22},{7,23},{8,24},{9,... | collective-permute-start | bytes 491528 | tf_op jit(solution)/shard_map/ppermute | solution.py:219
  46.3 0.0 collective-permute-done.6
  46.4 3.2 %collective-permute-start.7 = (bf16[2,160,256]{2,1,0:T(8,128)(2,1)S(1)}, bf16[2,160,256]{2,1,0:T(8,128)(2,1)S(1)}, u32[]{:S(2)}, u32[]{:S(2)}) collective-permute-start(bf16[2,160,256]{2,1,0:T(8,128)(2,1)S(1)} %add_convert_fusion), channel_id=1, source_target_pairs={{1,2},{2,1},{3,4},{4,3},{5,6},{6,5},{7,8},{8,7},{9,10},{10,9},{11,... | collective-permute-start | bytes 491528 | tf_op jit(solution)/shard_map/ppermute | solution.py:219
  49.6 1.2 %queries.1 = (bf16[160,256]{1,0:T(8,128)(2,1)}, bf16[160,256]{1,0:T(8,128)(2,1)}) custom-call(bf16[1280,256]{1,0:T(8,128)(2,1)S(1)} %get-tuple-element.30.ks, bf16[1280,256]{1,0:T(8,128)(2,1)S(1)} %get-tuple-element.31.vs, bf16[256,256]{1,0:T(8,128)(2,1)S(1)} %get-tuple-element.32.kc, bf16[256,256]{1,0:T(8,128)(2,1)S(1)} %get-tuple-element.33.vc, ...), custom_call_target="tpu_custom_call" | custom-call | flops 1000000000 | bytes 2097152 | tf_op jit(solution)/shard_map/queries/pallas_call | solution.py:192
  50.8 2.5 %collective-permute-done.9 = bf16[2,160,256]{2,1,0:T(8,128)(2,1)S(1)} collective-permute-done((bf16[2,160,256]{2,1,0:T(8,128)(2,1)S(1)}, bf16[2,160,256]{2,1,0:T(8,128)(2,1)S(1)}, u32[]{:S(2)}, u32[]{:S(2)}) %collective-permute-start.9) | collective-permute-done | bytes 163872 | tf_op jit(solution)/shard_map/ppermute | solution.py:219
  53.3 0.0 collective-permute-done.8
  53.3 4.4 %collective-permute-done.7 = bf16[2,160,256]{2,1,0:T(8,128)(2,1)S(1)} collective-permute-done((bf16[2,160,256]{2,1,0:T(8,128)(2,1)S(1)}, bf16[2,160,256]{2,1,0:T(8,128)(2,1)S(1)}, u32[]{:S(2)}, u32[]{:S(2)}) %collective-permute-start.7) | collective-permute-done | bytes 163872 | tf_op jit(solution)/shard_map/ppermute | solution.py:219
  57.8 0.1 fusion.9
  57.8 0.7 %fusion.10 = (bf16[1,160,256]{2,1,0:T(8,128)(2,1)}, bf16[1,160,256]{2,1,0:T(8,128)(2,1)}) fusion(bf16[2,160,256]{2,1,0:T(8,128)(2,1)S(1)} %fusion.9), kind=kLoop, calls=%fused_computation.17 | loop fusion | bytes 327680 | tf_op jit(solution)/shard_map/slice | solution.py:263
  (2 shorter events, 0.1 us)
Async XLA Ops:
  0.6 11.1 %copy-start = (bf16[1,2,80,256]{3,2,1,0:T(8,128)(2,1)S(1)}, bf16[1,2,80,256]{3,2,1,0:T(8,128)(2,1)}, u32[]{:S(2)}) copy-start(bf16[1,2,80,256]{3,2,1,0:T(8,128)(2,1)} %param.5) | copy-start | bytes 245764
  0.6 11.1 %copy-start.1 = (bf16[1,2,80,256]{3,2,1,0:T(8,128)(2,1)S(1)}, bf16[1,2,80,256]{3,2,1,0:T(8,128)(2,1)}, u32[]{:S(2)}) copy-start(bf16[1,2,80,256]{3,2,1,0:T(8,128)(2,1)} %param.8) | copy-start | bytes 245764
  1.6 11.4 %collective-permute-start.2 = (bf16[2,160,256]{2,1,0:T(8,128)(2,1)S(1)}, bf16[2,160,256]{2,1,0:T(8,128)(2,1)S(1)}, u32[]{:S(2)}, u32[]{:S(2)}) collective-permute-start(bf16[2,160,256]{2,1,0:T(8,128)(2,1)S(1)} %pad_maximum_fusion.1.x), channel_id=1, source_target_pairs={{1,2},{2,1},{3,4},{4,3},{5,6},{6,5},{7,8},{8,7},{9,10},{10,9},{11,... | collective-permute-start | bytes 491528 | tf_op jit(solution)/shard_map/ppermute | solution.py:219
  5.3 15.6 %collective-permute-start = (bf16[2,160,256]{2,1,0:T(8,128)(2,1)S(1)}, bf16[2,160,256]{2,1,0:T(8,128)(2,1)S(1)}, u32[]{:S(2)}, u32[]{:S(2)}) collective-permute-start(bf16[2,160,256]{2,1,0:T(8,128)(2,1)S(1)} %pad_maximum_fusion.1.x), channel_id=1, source_target_pairs={{16,32},{17,33},{18,34},{19,35},{20,36},{21,37},{22,38},{23,39},{2... | collective-permute-start | bytes 491528 | tf_op jit(solution)/shard_map/ppermute | solution.py:219
  8.6 12.4 %collective-permute-start.1 = (bf16[2,160,256]{2,1,0:T(8,128)(2,1)S(1)}, bf16[2,160,256]{2,1,0:T(8,128)(2,1)S(1)}, u32[]{:S(2)}, u32[]{:S(2)}) collective-permute-start(bf16[2,160,256]{2,1,0:T(8,128)(2,1)S(1)} %pad_maximum_fusion.1.x), channel_id=1, source_target_pairs={{0,16},{1,17},{2,18},{3,19},{4,20},{5,21},{6,22},{7,23},{8,24},{9,... | collective-permute-start | bytes 491528 | tf_op jit(solution)/shard_map/ppermute | solution.py:219
  11.8 0.7 %copy-start.2 = (s32[1,1,2,2]{3,2,1,0:T(2,128)S(1)}, s32[1,1,2,2]{3,2,1,0:T(2,128)}, u32[]{:S(2)}) copy-start(s32[1,1,2,2]{3,2,1,0:T(2,128)} %reach.1) | copy-start | bytes 52
  12.4 8.5 %copy-start.3 = (bf16[1,2,80,256]{3,2,1,0:T(8,128)(2,1)S(1)}, bf16[1,2,80,256]{3,2,1,0:T(8,128)(2,1)}, u32[]{:S(2)}) copy-start(bf16[1,2,80,256]{3,2,1,0:T(8,128)(2,1)} %param.7) | copy-start | bytes 245764
  12.4 8.5 %copy-start.4 = (bf16[1,2,80,256]{3,2,1,0:T(8,128)(2,1)S(1)}, bf16[1,2,80,256]{3,2,1,0:T(8,128)(2,1)}, u32[]{:S(2)}) copy-start(bf16[1,2,80,256]{3,2,1,0:T(8,128)(2,1)} %param.6) | copy-start | bytes 245764
  13.0 14.9 %collective-permute-start.3 = (bf16[2,160,256]{2,1,0:T(8,128)(2,1)S(1)}, bf16[2,160,256]{2,1,0:T(8,128)(2,1)S(1)}, u32[]{:S(2)}, u32[]{:S(2)}) collective-permute-start(bf16[2,160,256]{2,1,0:T(8,128)(2,1)S(1)} %collective-permute-done.2.xo), channel_id=1, source_target_pairs={{16,32},{17,33},{18,34},{19,35},{20,36},{21,37},{22,38},{23,39},{2... | collective-permute-start | bytes 491528 | tf_op jit(solution)/shard_map/ppermute | solution.py:219
  19.0 8.9 %collective-permute-start.4 = (bf16[2,160,256]{2,1,0:T(8,128)(2,1)S(1)}, bf16[2,160,256]{2,1,0:T(8,128)(2,1)S(1)}, u32[]{:S(2)}, u32[]{:S(2)}) collective-permute-start(bf16[2,160,256]{2,1,0:T(8,128)(2,1)S(1)} %collective-permute-done.2.xo), channel_id=1, source_target_pairs={{0,16},{1,17},{2,18},{3,19},{4,20},{5,21},{6,22},{7,23},{8,24},{9,... | collective-permute-start | bytes 491528 | tf_op jit(solution)/shard_map/ppermute | solution.py:219
  29.6 9.6 %collective-permute-start.5 = (bf16[2,160,256]{2,1,0:T(8,128)(2,1)S(1)}, bf16[2,160,256]{2,1,0:T(8,128)(2,1)S(1)}, u32[]{:S(2)}, u32[]{:S(2)}) collective-permute-start(bf16[2,160,256]{2,1,0:T(8,128)(2,1)S(1)} %get-tuple-element.43), channel_id=1, source_target_pairs={{1,2},{2,1},{3,4},{4,3},{5,6},{6,5},{7,8},{8,7},{9,10},{10,9},{11,... | collective-permute-start | bytes 491528 | tf_op jit(solution)/shard_map/ppermute | solution.py:219
  37.2 9.1 %collective-permute-start.6 = (bf16[2,160,256]{2,1,0:T(8,128)(2,1)S(1)}, bf16[2,160,256]{2,1,0:T(8,128)(2,1)S(1)}, u32[]{:S(2)}, u32[]{:S(2)}) collective-permute-start(bf16[2,160,256]{2,1,0:T(8,128)(2,1)S(1)} %get-tuple-element.47), channel_id=1, source_target_pairs={{0,16},{1,17},{2,18},{3,19},{4,20},{5,21},{6,22},{7,23},{8,24},{9,... | collective-permute-start | bytes 491528 | tf_op jit(solution)/shard_map/ppermute | solution.py:219
  39.3 14.1 %collective-permute-start.9 = (bf16[2,160,256]{2,1,0:T(8,128)(2,1)S(1)}, bf16[2,160,256]{2,1,0:T(8,128)(2,1)S(1)}, u32[]{:S(2)}, u32[]{:S(2)}) collective-permute-start(bf16[2,160,256]{2,1,0:T(8,128)(2,1)S(1)} %fusion.4), channel_id=1, source_target_pairs={{16,32},{17,33},{18,34},{19,35},{20,36},{21,37},{22,38},{23,39},{2... | collective-permute-start | bytes 491528 | tf_op jit(solution)/shard_map/ppermute | solution.py:219
  44.4 8.9 %collective-permute-start.8 = (bf16[2,160,256]{2,1,0:T(8,128)(2,1)S(1)}, bf16[2,160,256]{2,1,0:T(8,128)(2,1)S(1)}, u32[]{:S(2)}, u32[]{:S(2)}) collective-permute-start(bf16[2,160,256]{2,1,0:T(8,128)(2,1)S(1)} %fusion.1), channel_id=1, source_target_pairs={{0,16},{1,17},{2,18},{3,19},{4,20},{5,21},{6,22},{7,23},{8,24},{9,... | collective-permute-start | bytes 491528 | tf_op jit(solution)/shard_map/ppermute | solution.py:219
  46.4 11.4 %collective-permute-start.7 = (bf16[2,160,256]{2,1,0:T(8,128)(2,1)S(1)}, bf16[2,160,256]{2,1,0:T(8,128)(2,1)S(1)}, u32[]{:S(2)}, u32[]{:S(2)}) collective-permute-start(bf16[2,160,256]{2,1,0:T(8,128)(2,1)S(1)} %add_convert_fusion), channel_id=1, source_target_pairs={{1,2},{2,1},{3,4},{4,3},{5,6},{6,5},{7,8},{8,7},{9,10},{10,9},{11,... | collective-permute-start | bytes 491528 | tf_op jit(solution)/shard_map/ppermute | solution.py:219

commit v3 on v2

--- a/solution.py
+++ b/solution.py
@@ -86,7 +86,7 @@
 
 
 def softmax_kernel(
-    qs, os_, bias, x, xf, xe, xo, xfo, xeo, xp,
+    qs, os_, bias, x, xf, xe, xo, xeo, xfo, xp,
     gfo_, pm, gm, pc, gc, ks, vs, kc, vc,
     sm, dm, sc, dc,
 ):
@@ -227,8 +227,8 @@
     xf = swap(x, fo)
     xo = swap(x, ho)
     xe = swap(x, fe)
-    xfo = swap(xo, fo)
     xeo = swap(xo, fe)
+    xfo = swap(xf, ho)
     xp = share(jnp.concatenate([x, xf, xe]))
     keys_all, keys_corner = (BLOCKS * BLOCK, CHANS), (TILE, CHANS)
     main, corner = (HEADS, TOK, 2 * BLOCK), (HEADS, TOK, TILE)
@@ -237,7 +237,7 @@
         [(tile, BF16)] * 2 + [((HEADS, 8, BLOCK), F32)], (), 1,
     )
     gfo_, pm, gm, pc, gc, ks, vs, kc, vc = call(
-        softmax_kernel, "softmax", 2 * 10**9, (qs, os_, bias, x, xf, xe, xo, xfo, xeo, xp),
+        softmax_kernel, "softmax", 2 * 10**9, (qs, os_, bias, x, xf, xe, xo, xeo, xfo, xp),
         [(pair, BF16)] + [(main, BF16)] * 2 + [(corner, BF16)] * 2
         + [(keys_all, BF16)] * 2 + [(keys_corner, BF16)] * 2,
         [((TOK, 2 * BLOCK), F32)] * 2 + [((TOK, TILE), F32)] * 2,

time: 58.9 us -> 58.8 us (level)
  the two profiles are of different devices: /device:TPU:321 before, /device:TPU:193 now
where the time goes in v3:
time: 58.8 us; the launch traced here: 58.4 us
  starting transfers between devices  30.7 us (52%)
  waiting for transfers between devices  15 us (26%)
  blocking collectives  5.02 us (9%)
  Pallas kernels  4.03 us (7%)
  other arithmetic  1.36 us (2%)
  local copies, waits for them, and re-layouts  1.34 us (2%)
  between operations  0.88 us (1%)
    ppermute x10, starting transfers between devices, local(): swap = lambda array, pairs: lax.ppermute(array, BOTH, pairs)  30.7 us
    ppermute x10, waiting for transfers between devices, local(): swap = lambda array, pairs: lax.ppermute(array, BOTH, pairs)  15 us
    all_gather x2, blocking collectives, local(): share = lambda v: lax.all_gather(v, BOTH, axis_index_groups=chip)  5.02 us
    pallas_call x4, Pallas kernels, call(): pl.pallas_call(body, out_shape=tuple((jax.ShapeDtypeStruct(shape, kind) f...  4.03 us
  transfers between devices with their start and end apart: 10, of which 4 were waited for; matrix products, arithmetic and copies ran while one was open for 0% of the time, Pallas kernels for 4%

profile of v3, /device:TPU:193, one launch (start us, length us, event | category | flops | bytes accessed | tf_op | source)
XLA Modules:
  0.0 58.4 jit_solution(14309271582855567651)
XLA Ops:
  0.6 0.0 copy-start
  0.6 0.0 copy-start.1
  0.7 1.0 %pad_maximum_fusion.1.x = bf16[2,160,256]{2,1,0:T(8,128)(2,1)S(1)} fusion(bf16[1,160,256]{2,1,0:T(8,128)(2,1)} %bitcast.40, bf16[1,160,256]{2,1,0:T(8,128)(2,1)} %bitcast.42), kind=kLoop, calls=%fused_computation.16 | loop fusion | flops 81920 | bytes 327680 | tf_op jit(solution)/shard_map/stack | solution.py:226
  1.6 2.8 %collective-permute-start.2 = (bf16[2,160,256]{2,1,0:T(8,128)(2,1)S(1)}, bf16[2,160,256]{2,1,0:T(8,128)(2,1)S(1)}, u32[]{:S(2)}, u32[]{:S(2)}) collective-permute-start(bf16[2,160,256]{2,1,0:T(8,128)(2,1)S(1)} %pad_maximum_fusion.1.x), channel_id=1, source_target_pairs={{1,2},{2,1},{3,4},{4,3},{5,6},{6,5},{7,8},{8,7},{9,10},{10,9},{11,... | collective-permute-start | bytes 491528 | tf_op jit(solution)/shard_map/ppermute | solution.py:219
  4.4 3.3 %collective-permute-start = (bf16[2,160,256]{2,1,0:T(8,128)(2,1)S(1)}, bf16[2,160,256]{2,1,0:T(8,128)(2,1)S(1)}, u32[]{:S(2)}, u32[]{:S(2)}) collective-permute-start(bf16[2,160,256]{2,1,0:T(8,128)(2,1)S(1)} %pad_maximum_fusion.1.x), channel_id=1, source_target_pairs={{16,32},{17,33},{18,34},{19,35},{20,36},{21,37},{22,38},{23,39},{2... | collective-permute-start | bytes 491528 | tf_op jit(solution)/shard_map/ppermute | solution.py:219
  7.7 3.2 %collective-permute-start.1 = (bf16[2,160,256]{2,1,0:T(8,128)(2,1)S(1)}, bf16[2,160,256]{2,1,0:T(8,128)(2,1)S(1)}, u32[]{:S(2)}, u32[]{:S(2)}) collective-permute-start(bf16[2,160,256]{2,1,0:T(8,128)(2,1)S(1)} %pad_maximum_fusion.1.x), channel_id=1, source_target_pairs={{0,16},{1,17},{2,18},{3,19},{4,20},{5,21},{6,22},{7,23},{8,24},{9,... | collective-permute-start | bytes 491528 | tf_op jit(solution)/shard_map/ppermute | solution.py:219
  10.9 0.0 copy-start.2
  10.9 0.0 copy-done
  10.9 0.0 copy-done.1
  10.9 0.7 %copy-done.2 = s32[1,1,2,2]{3,2,1,0:T(2,128)S(1)} copy-done((s32[1,1,2,2]{3,2,1,0:T(2,128)S(1)}, s32[1,1,2,2]{3,2,1,0:T(2,128)}, u32[]{:S(2)}) %copy-start.2) | copy-done | bytes 40
  11.6 0.0 copy-start.3
  11.6 0.0 copy-start.4
  11.6 0.6 prepare.1
  12.1 0.0 collective-permute-done.2.xo
  12.2 2.2 %collective-permute-start.3 = (bf16[2,160,256]{2,1,0:T(8,128)(2,1)S(1)}, bf16[2,160,256]{2,1,0:T(8,128)(2,1)S(1)}, u32[]{:S(2)}, u32[]{:S(2)}) collective-permute-start(bf16[2,160,256]{2,1,0:T(8,128)(2,1)S(1)} %collective-permute-done.2.xo), channel_id=1, source_target_pairs={{0,16},{1,17},{2,18},{3,19},{4,20},{5,21},{6,22},{7,23},{8,24},{9,... | collective-permute-start | bytes 491528 | tf_op jit(solution)/shard_map/ppermute | solution.py:219
  14.3 3.5 %collective-permute-done.xf = bf16[2,160,256]{2,1,0:T(8,128)(2,1)S(1)} collective-permute-done((bf16[2,160,256]{2,1,0:T(8,128)(2,1)S(1)}, bf16[2,160,256]{2,1,0:T(8,128)(2,1)S(1)}, u32[]{:S(2)}, u32[]{:S(2)}) %collective-permute-start) | collective-permute-done | bytes 163872 | tf_op jit(solution)/shard_map/ppermute | solution.py:219
  17.8 4.7 %collective-permute-start.4 = (bf16[2,160,256]{2,1,0:T(8,128)(2,1)S(1)}, bf16[2,160,256]{2,1,0:T(8,128)(2,1)S(1)}, u32[]{:S(2)}, u32[]{:S(2)}) collective-permute-start(bf16[2,160,256]{2,1,0:T(8,128)(2,1)S(1)} %collective-permute-done.xf), channel_id=1, source_target_pairs={{1,2},{2,1},{3,4},{4,3},{5,6},{6,5},{7,8},{8,7},{9,10},{10,9},{11,... | collective-permute-start | bytes 491528 | tf_op jit(solution)/shard_map/ppermute | solution.py:219
  22.4 0.0 collective-permute-done.1.xe
  22.5 0.0 copy-done.3
  22.5 0.0 copy-done.4
  22.5 0.1 pad_maximum_fusion
  22.5 2.5 %all-gather = bf16[12,160,256]{2,1,0:T(8,128)(2,1)S(1)} all-gather(bf16[6,160,256]{2,1,0:T(8,128)(2,1)S(1)} %pad_maximum_fusion), channel_id=2, replica_groups={{0,1},{2,3},{4,5},{6,7},{8,9},{10,11},{12,13},{14,15},{16,17},{18,19},{..., dimensions={0}, use_global_device_ids=true | all-gather | bytes 1474560 | tf_op jit(solution)/shard_map/all_gather | solution.py:221
  25.0 0.0 collective-permute-done.3.xeo
  25.1 1.9 %collective-permute-done.4.xfo = bf16[2,160,256]{2,1,0:T(8,128)(2,1)S(1)} collective-permute-done((bf16[2,160,256]{2,1,0:T(8,128)(2,1)S(1)}, bf16[2,160,256]{2,1,0:T(8,128)(2,1)S(1)}, u32[]{:S(2)}, u32[]{:S(2)}) %collective-permute-start.4) | collective-permute-done | bytes 163872 | tf_op jit(solution)/shard_map/ppermute | solution.py:219
  26.9 1.7 %softmax.1 = (bf16[2,160,256]{2,1,0:T(8,128)(2,1)S(1)}, bf16[2,160,512]{2,1,0:T(8,128)(2,1)S(1)}, bf16[2,160,512]{2,1,0:T(8,128)(2,1)S(1)}, bf16[2,160,256]{2,1,...) custom-call(bf16[160,256]{1,0:T(8,128)(2,1)S(1)} %get-tuple-element., ...), custom_call_target="tpu_custom_call" | custom-call | flops 2000000000 | bytes 2097152 | tf_op jit(solution)/shard_map/softmax/pallas_call | solution.py:192
  28.6 3.6 %collective-permute-start.5 = (bf16[2,160,256]{2,1,0:T(8,128)(2,1)S(1)}, bf16[2,160,256]{2,1,0:T(8,128)(2,1)S(1)}, u32[]{:S(2)}, u32[]{:S(2)}) collective-permute-start(bf16[2,160,256]{2,1,0:T(8,128)(2,1)S(1)} %get-tuple-element.43), channel_id=1, source_target_pairs={{1,2},{2,1},{3,4},{4,3},{5,6},{6,5},{7,8},{8,7},{9,10},{10,9},{11,... | collective-permute-start | bytes 491528 | tf_op jit(solution)/shard_map/ppermute | solution.py:219
  32.2 0.6 keys.1
  32.8 2.5 %all-gather.1 = bf16[12,160,256]{2,1,0:T(8,128)(2,1)S(1)} all-gather(bf16[6,160,256]{2,1,0:T(8,128)(2,1)S(1)} %get-tuple-element.41), channel_id=3, replica_groups={{0,1},{2,3},{4,5},{6,7},{8,9},{10,11},{12,13},{14,15},{16,17},{18,19},{..., dimensions={0}, use_global_device_ids=true | all-gather | bytes 1474560 | tf_op jit(solution)/shard_map/all_gather | solution.py:221
  35.3 1.9 %collective-permute-start.6 = (bf16[2,160,256]{2,1,0:T(8,128)(2,1)S(1)}, bf16[2,160,256]{2,1,0:T(8,128)(2,1)S(1)}, u32[]{:S(2)}, u32[]{:S(2)}) collective-permute-start(bf16[2,160,256]{2,1,0:T(8,128)(2,1)S(1)} %get-tuple-element.47), channel_id=1, source_target_pairs={{0,16},{1,17},{2,18},{3,19},{4,20},{5,21},{6,22},{7,23},{8,24},{9,... | collective-permute-start | bytes 491528 | tf_op jit(solution)/shard_map/ppermute | solution.py:219
  37.2 0.1 dynamic-slice_convert_fusion
  37.3 0.0 collective-permute-done.5
  37.3 0.1 fusion.4
  37.4 3.9 %collective-permute-start.9 = (bf16[2,160,256]{2,1,0:T(8,128)(2,1)S(1)}, bf16[2,160,256]{2,1,0:T(8,128)(2,1)S(1)}, u32[]{:S(2)}, u32[]{:S(2)}) collective-permute-start(bf16[2,160,256]{2,1,0:T(8,128)(2,1)S(1)} %fusion.4), channel_id=1, source_target_pairs={{16,32},{17,33},{18,34},{19,35},{20,36},{21,37},{22,38},{23,39},{2... | collective-permute-start | bytes 491528 | tf_op jit(solution)/shard_map/ppermute | solution.py:219
  41.3 1.9 %collective-permute-start.8 = (bf16[2,160,256]{2,1,0:T(8,128)(2,1)S(1)}, bf16[2,160,256]{2,1,0:T(8,128)(2,1)S(1)}, u32[]{:S(2)}, u32[]{:S(2)}) collective-permute-start(bf16[2,160,256]{2,1,0:T(8,128)(2,1)S(1)} %fusion.1), channel_id=1, source_target_pairs={{0,16},{1,17},{2,18},{3,19},{4,20},{5,21},{6,22},{7,23},{8,24},{9,... | collective-permute-start | bytes 491528 | tf_op jit(solution)/shard_map/ppermute | solution.py:219
  43.3 0.0 collective-permute-done.6
  43.3 3.4 %collective-permute-start.7 = (bf16[2,160,256]{2,1,0:T(8,128)(2,1)S(1)}, bf16[2,160,256]{2,1,0:T(8,128)(2,1)S(1)}, u32[]{:S(2)}, u32[]{:S(2)}) collective-permute-start(bf16[2,160,256]{2,1,0:T(8,128)(2,1)S(1)} %add_convert_fusion), channel_id=1, source_target_pairs={{1,2},{2,1},{3,4},{4,3},{5,6},{6,5},{7,8},{8,7},{9,10},{10,9},{11,... | collective-permute-start | bytes 491528 | tf_op jit(solution)/shard_map/ppermute | solution.py:219
  46.7 1.2 %queries.1 = (bf16[160,256]{1,0:T(8,128)(2,1)}, bf16[160,256]{1,0:T(8,128)(2,1)}) custom-call(bf16[1280,256]{1,0:T(8,128)(2,1)S(1)} %get-tuple-element.30.ks, bf16[1280,256]{1,0:T(8,128)(2,1)S(1)} %get-tuple-element.31.vs, bf16[256,256]{1,0:T(8,128)(2,1)S(1)} %get-tuple-element.32.kc, bf16[256,256]{1,0:T(8,128)(2,1)S(1)} %get-tuple-element.33.vc, ...), custom_call_target="tpu_custom_call" | custom-call | flops 1000000000 | bytes 2097152 | tf_op jit(solution)/shard_map/queries/pallas_call | solution.py:192
  47.9 3.1 %collective-permute-done.9 = bf16[2,160,256]{2,1,0:T(8,128)(2,1)S(1)} collective-permute-done((bf16[2,160,256]{2,1,0:T(8,128)(2,1)S(1)}, bf16[2,160,256]{2,1,0:T(8,128)(2,1)S(1)}, u32[]{:S(2)}, u32[]{:S(2)}) %collective-permute-start.9) | collective-permute-done | bytes 163872 | tf_op jit(solution)/shard_map/ppermute | solution.py:219
  51.0 0.0 collective-permute-done.8
  51.0 6.6 %collective-permute-done.7 = bf16[2,160,256]{2,1,0:T(8,128)(2,1)S(1)} collective-permute-done((bf16[2,160,256]{2,1,0:T(8,128)(2,1)S(1)}, bf16[2,160,256]{2,1,0:T(8,128)(2,1)S(1)}, u32[]{:S(2)}, u32[]{:S(2)}) %collective-permute-start.7) | collective-permute-done | bytes 163872 | tf_op jit(solution)/shard_map/ppermute | solution.py:219
  57.6 0.1 fusion.9
  57.7 0.7 %fusion.10 = (bf16[1,160,256]{2,1,0:T(8,128)(2,1)}, bf16[1,160,256]{2,1,0:T(8,128)(2,1)}) fusion(bf16[2,160,256]{2,1,0:T(8,128)(2,1)S(1)} %fusion.9), kind=kLoop, calls=%fused_computation.17 | loop fusion | bytes 327680 | tf_op jit(solution)/shard_map/slice | solution.py:263
  (2 shorter events, 0.1 us)
Async XLA Ops:
  0.6 10.3 %copy-start = (bf16[1,2,80,256]{3,2,1,0:T(8,128)(2,1)S(1)}, bf16[1,2,80,256]{3,2,1,0:T(8,128)(2,1)}, u32[]{:S(2)}) copy-start(bf16[1,2,80,256]{3,2,1,0:T(8,128)(2,1)} %param.5) | copy-start | bytes 245764
  0.6 10.3 %copy-start.1 = (bf16[1,2,80,256]{3,2,1,0:T(8,128)(2,1)S(1)}, bf16[1,2,80,256]{3,2,1,0:T(8,128)(2,1)}, u32[]{:S(2)}) copy-start(bf16[1,2,80,256]{3,2,1,0:T(8,128)(2,1)} %param.8) | copy-start | bytes 245764
  1.6 10.5 %collective-permute-start.2 = (bf16[2,160,256]{2,1,0:T(8,128)(2,1)S(1)}, bf16[2,160,256]{2,1,0:T(8,128)(2,1)S(1)}, u32[]{:S(2)}, u32[]{:S(2)}) collective-permute-start(bf16[2,160,256]{2,1,0:T(8,128)(2,1)S(1)} %pad_maximum_fusion.1.x), channel_id=1, source_target_pairs={{1,2},{2,1},{3,4},{4,3},{5,6},{6,5},{7,8},{8,7},{9,10},{10,9},{11,... | collective-permute-start | bytes 491528 | tf_op jit(solution)/shard_map/ppermute | solution.py:219
  4.4 13.4 %collective-permute-start = (bf16[2,160,256]{2,1,0:T(8,128)(2,1)S(1)}, bf16[2,160,256]{2,1,0:T(8,128)(2,1)S(1)}, u32[]{:S(2)}, u32[]{:S(2)}) collective-permute-start(bf16[2,160,256]{2,1,0:T(8,128)(2,1)S(1)} %pad_maximum_fusion.1.x), channel_id=1, source_target_pairs={{16,32},{17,33},{18,34},{19,35},{20,36},{21,37},{22,38},{23,39},{2... | collective-permute-start | bytes 491528 | tf_op jit(solution)/shard_map/ppermute | solution.py:219
  7.7 14.7 %collective-permute-start.1 = (bf16[2,160,256]{2,1,0:T(8,128)(2,1)S(1)}, bf16[2,160,256]{2,1,0:T(8,128)(2,1)S(1)}, u32[]{:S(2)}, u32[]{:S(2)}) collective-permute-start(bf16[2,160,256]{2,1,0:T(8,128)(2,1)S(1)} %pad_maximum_fusion.1.x), channel_id=1, source_target_pairs={{0,16},{1,17},{2,18},{3,19},{4,20},{5,21},{6,22},{7,23},{8,24},{9,... | collective-permute-start | bytes 491528 | tf_op jit(solution)/shard_map/ppermute | solution.py:219
  10.9 0.7 %copy-start.2 = (s32[1,1,2,2]{3,2,1,0:T(2,128)S(1)}, s32[1,1,2,2]{3,2,1,0:T(2,128)}, u32[]{:S(2)}) copy-start(s32[1,1,2,2]{3,2,1,0:T(2,128)} %reach.1) | copy-start | bytes 52
  11.6 10.9 %copy-start.3 = (bf16[1,2,80,256]{3,2,1,0:T(8,128)(2,1)S(1)}, bf16[1,2,80,256]{3,2,1,0:T(8,128)(2,1)}, u32[]{:S(2)}) copy-start(bf16[1,2,80,256]{3,2,1,0:T(8,128)(2,1)} %param.7) | copy-start | bytes 245764
  11.6 10.9 %copy-start.4 = (bf16[1,2,80,256]{3,2,1,0:T(8,128)(2,1)S(1)}, bf16[1,2,80,256]{3,2,1,0:T(8,128)(2,1)}, u32[]{:S(2)}) copy-start(bf16[1,2,80,256]{3,2,1,0:T(8,128)(2,1)} %param.6) | copy-start | bytes 245764
  12.2 12.9 %collective-permute-start.3 = (bf16[2,160,256]{2,1,0:T(8,128)(2,1)S(1)}, bf16[2,160,256]{2,1,0:T(8,128)(2,1)S(1)}, u32[]{:S(2)}, u32[]{:S(2)}) collective-permute-start(bf16[2,160,256]{2,1,0:T(8,128)(2,1)S(1)} %collective-permute-done.2.xo), channel_id=1, source_target_pairs={{0,16},{1,17},{2,18},{3,19},{4,20},{5,21},{6,22},{7,23},{8,24},{9,... | collective-permute-start | bytes 491528 | tf_op jit(solution)/shard_map/ppermute | solution.py:219
  17.8 9.1 %collective-permute-start.4 = (bf16[2,160,256]{2,1,0:T(8,128)(2,1)S(1)}, bf16[2,160,256]{2,1,0:T(8,128)(2,1)S(1)}, u32[]{:S(2)}, u32[]{:S(2)}) collective-permute-start(bf16[2,160,256]{2,1,0:T(8,128)(2,1)S(1)} %collective-permute-done.xf), channel_id=1, source_target_pairs={{1,2},{2,1},{3,4},{4,3},{5,6},{6,5},{7,8},{8,7},{9,10},{10,9},{11,... | collective-permute-start | bytes 491528 | tf_op jit(solution)/shard_map/ppermute | solution.py:219
  28.6 8.7 %collective-permute-start.5 = (bf16[2,160,256]{2,1,0:T(8,128)(2,1)S(1)}, bf16[2,160,256]{2,1,0:T(8,128)(2,1)S(1)}, u32[]{:S(2)}, u32[]{:S(2)}) collective-permute-start(bf16[2,160,256]{2,1,0:T(8,128)(2,1)S(1)} %get-tuple-element.43), channel_id=1, source_target_pairs={{1,2},{2,1},{3,4},{4,3},{5,6},{6,5},{7,8},{8,7},{9,10},{10,9},{11,... | collective-permute-start | bytes 491528 | tf_op jit(solution)/shard_map/ppermute | solution.py:219
  35.3 8.0 %collective-permute-start.6 = (bf16[2,160,256]{2,1,0:T(8,128)(2,1)S(1)}, bf16[2,160,256]{2,1,0:T(8,128)(2,1)S(1)}, u32[]{:S(2)}, u32[]{:S(2)}) collective-permute-start(bf16[2,160,256]{2,1,0:T(8,128)(2,1)S(1)} %get-tuple-element.47), channel_id=1, source_target_pairs={{0,16},{1,17},{2,18},{3,19},{4,20},{5,21},{6,22},{7,23},{8,24},{9,... | collective-permute-start | bytes 491528 | tf_op jit(solution)/shard_map/ppermute | solution.py:219
  37.4 13.7 %collective-permute-start.9 = (bf16[2,160,256]{2,1,0:T(8,128)(2,1)S(1)}, bf16[2,160,256]{2,1,0:T(8,128)(2,1)S(1)}, u32[]{:S(2)}, u32[]{:S(2)}) collective-permute-start(bf16[2,160,256]{2,1,0:T(8,128)(2,1)S(1)} %fusion.4), channel_id=1, source_target_pairs={{16,32},{17,33},{18,34},{19,35},{20,36},{21,37},{22,38},{23,39},{2... | collective-permute-start | bytes 491528 | tf_op jit(solution)/shard_map/ppermute | solution.py:219
  41.3 9.7 %collective-permute-start.8 = (bf16[2,160,256]{2,1,0:T(8,128)(2,1)S(1)}, bf16[2,160,256]{2,1,0:T(8,128)(2,1)S(1)}, u32[]{:S(2)}, u32[]{:S(2)}) collective-permute-start(bf16[2,160,256]{2,1,0:T(8,128)(2,1)S(1)} %fusion.1), channel_id=1, source_target_pairs={{0,16},{1,17},{2,18},{3,19},{4,20},{5,21},{6,22},{7,23},{8,24},{9,... | collective-permute-start | bytes 491528 | tf_op jit(solution)/shard_map/ppermute | solution.py:219
  43.3 14.3 %collective-permute-start.7 = (bf16[2,160,256]{2,1,0:T(8,128)(2,1)S(1)}, bf16[2,160,256]{2,1,0:T(8,128)(2,1)S(1)}, u32[]{:S(2)}, u32[]{:S(2)}) collective-permute-start(bf16[2,160,256]{2,1,0:T(8,128)(2,1)S(1)} %add_convert_fusion), channel_id=1, source_target_pairs={{1,2},{2,1},{3,4},{4,3},{5,6},{6,5},{7,8},{8,7},{9,10},{10,9},{11,... | collective-permute-start | bytes 491528 | tf_op jit(solution)/shard_map/ppermute | solution.py:219

commit v4 on v3

--- a/solution.py
+++ b/solution.py
@@ -232,6 +232,7 @@
     xp = share(jnp.concatenate([x, xf, xe]))
     keys_all, keys_corner = (BLOCKS * BLOCK, CHANS), (TILE, CHANS)
     main, corner = (HEADS, TOK, 2 * BLOCK), (HEADS, TOK, TILE)
+    reach, q, o, xeo = lax.optimization_barrier((reach, q, o, xeo))
     qs, os_, bias = call(
         functools.partial(prepare_kernel, nframe, nheight), "prepare", 10**8, (reach, q, o),
         [(tile, BF16)] * 2 + [((HEADS, 8, BLOCK), F32)], (), 1,

time: 58.8 us -> 58.8 us (level)
  waiting for transfers between devices: 15 us -> 14 us
  starting transfers between devices: 30.7 us -> 31.6 us
    ppermute x10, waiting for transfers between devices: 15 us -> 14 us  [local(): swap = lambda array, pairs: lax.ppermute(array, BOTH, pairs)]
    ppermute x10, starting transfers between devices: 30.7 us -> 31.6 us  [local(): swap = lambda array, pairs: lax.ppermute(array, BOTH, pairs)]
where the time goes in v4:
time: 58.8 us; the launch traced here: 58.4 us
  starting transfers between devices  31.6 us (54%)
  waiting for transfers between devices  14 us (24%)
  blocking collectives  5.15 us (9%)
  Pallas kernels  4.04 us (7%)
  local copies, waits for them, and re-layouts  1.36 us (2%)
  other arithmetic  1.36 us (2%)
  between operations  0.88 us (1%)
    ppermute x10, starting transfers between devices, local(): swap = lambda array, pairs: lax.ppermute(array, BOTH, pairs)  31.6 us
    ppermute x10, waiting for transfers between devices, local(): swap = lambda array, pairs: lax.ppermute(array, BOTH, pairs)  14 us
    all_gather x2, blocking collectives, local(): share = lambda v: lax.all_gather(v, BOTH, axis_index_groups=chip)  5.15 us
    pallas_call x4, Pallas kernels, call(): pl.pallas_call(body, out_shape=tuple((jax.ShapeDtypeStruct(shape, kind) f...  4.04 us
  transfers between devices with their start and end apart: 10, of which 4 were waited for; matrix products, arithmetic and copies ran while one was open for 0% of the time, Pallas kernels for 4%

profile of v4, /device:TPU:193, one launch (start us, length us, event | category | flops | bytes accessed | tf_op | source)
XLA Modules:
  0.0 58.4 jit_solution(2544172139359178141)
XLA Ops:
  0.6 0.0 copy-start.3
  0.6 0.0 copy-start.4
  0.7 1.0 %pad_maximum_fusion.1.x = bf16[2,160,256]{2,1,0:T(8,128)(2,1)S(1)} fusion(bf16[1,160,256]{2,1,0:T(8,128)(2,1)} %bitcast.40, bf16[1,160,256]{2,1,0:T(8,128)(2,1)} %bitcast.42), kind=kLoop, calls=%fused_computation.16 | loop fusion | flops 81920 | bytes 327680 | tf_op jit(solution)/shard_map/stack | solution.py:226
  1.6 2.8 %collective-permute-start = (bf16[2,160,256]{2,1,0:T(8,128)(2,1)S(1)}, bf16[2,160,256]{2,1,0:T(8,128)(2,1)S(1)}, u32[]{:S(2)}, u32[]{:S(2)}) collective-permute-start(bf16[2,160,256]{2,1,0:T(8,128)(2,1)S(1)} %pad_maximum_fusion.1.x), channel_id=1, source_target_pairs={{1,2},{2,1},{3,4},{4,3},{5,6},{6,5},{7,8},{8,7},{9,10},{10,9},{11,... | collective-permute-start | bytes 491528 | tf_op jit(solution)/shard_map/ppermute | solution.py:219
  4.4 3.3 %collective-permute-start.2 = (bf16[2,160,256]{2,1,0:T(8,128)(2,1)S(1)}, bf16[2,160,256]{2,1,0:T(8,128)(2,1)S(1)}, u32[]{:S(2)}, u32[]{:S(2)}) collective-permute-start(bf16[2,160,256]{2,1,0:T(8,128)(2,1)S(1)} %pad_maximum_fusion.1.x), channel_id=1, source_target_pairs={{16,32},{17,33},{18,34},{19,35},{20,36},{21,37},{22,38},{23,39},{2... | collective-permute-start | bytes 491528 | tf_op jit(solution)/shard_map/ppermute | solution.py:219
  7.7 3.2 %collective-permute-start.3 = (bf16[2,160,256]{2,1,0:T(8,128)(2,1)S(1)}, bf16[2,160,256]{2,1,0:T(8,128)(2,1)S(1)}, u32[]{:S(2)}, u32[]{:S(2)}) collective-permute-start(bf16[2,160,256]{2,1,0:T(8,128)(2,1)S(1)} %pad_maximum_fusion.1.x), channel_id=1, source_target_pairs={{0,16},{1,17},{2,18},{3,19},{4,20},{5,21},{6,22},{7,23},{8,24},{9,... | collective-permute-start | bytes 491528 | tf_op jit(solution)/shard_map/ppermute | solution.py:219
  10.9 0.0 collective-permute-done.xo
  10.9 3.2 %collective-permute-start.1 = (bf16[2,160,256]{2,1,0:T(8,128)(2,1)S(1)}, bf16[2,160,256]{2,1,0:T(8,128)(2,1)S(1)}, u32[]{:S(2)}, u32[]{:S(2)}) collective-permute-start(bf16[2,160,256]{2,1,0:T(8,128)(2,1)S(1)} %collective-permute-done.xo), channel_id=1, source_target_pairs={{0,16},{1,17},{2,18},{3,19},{4,20},{5,21},{6,22},{7,23},{8,24},{9,... | collective-permute-start | bytes 491528 | tf_op jit(solution)/shard_map/ppermute | solution.py:219
  14.1 3.7 %collective-permute-done.2.xf = bf16[2,160,256]{2,1,0:T(8,128)(2,1)S(1)} collective-permute-done((bf16[2,160,256]{2,1,0:T(8,128)(2,1)S(1)}, bf16[2,160,256]{2,1,0:T(8,128)(2,1)S(1)}, u32[]{:S(2)}, u32[]{:S(2)}) %collective-permute-start.2) | collective-permute-done | bytes 163872 | tf_op jit(solution)/shard_map/ppermute | solution.py:219
  17.8 4.7 %collective-permute-start.4 = (bf16[2,160,256]{2,1,0:T(8,128)(2,1)S(1)}, bf16[2,160,256]{2,1,0:T(8,128)(2,1)S(1)}, u32[]{:S(2)}, u32[]{:S(2)}) collective-permute-start(bf16[2,160,256]{2,1,0:T(8,128)(2,1)S(1)} %collective-permute-done.2.xf), channel_id=1, source_target_pairs={{1,2},{2,1},{3,4},{4,3},{5,6},{6,5},{7,8},{8,7},{9,10},{10,9},{11,... | collective-permute-start | bytes 491528 | tf_op jit(solution)/shard_map/ppermute | solution.py:219
  22.4 0.0 collective-permute-done.3.xe
  22.5 0.0 copy-done.3
  22.5 0.0 copy-done.4
  22.5 0.1 pad_maximum_fusion
  22.5 0.0 copy-start
  22.5 0.0 copy-start.1
  22.6 2.6 %all-gather = bf16[12,160,256]{2,1,0:T(8,128)(2,1)S(1)} all-gather(bf16[6,160,256]{2,1,0:T(8,128)(2,1)S(1)} %pad_maximum_fusion), channel_id=2, replica_groups={{0,1},{2,3},{4,5},{6,7},{8,9},{10,11},{12,13},{14,15},{16,17},{18,19},{..., dimensions={0}, use_global_device_ids=true | all-gather | bytes 1474560 | tf_op jit(solution)/shard_map/all_gather | solution.py:221
  25.2 0.0 collective-permute-done.1.xeo
  25.2 0.0 copy-start.2
  25.2 0.0 copy-done
  25.2 0.0 copy-done.1
  25.2 0.7 %copy-done.2 = s32[1,1,2,2]{3,2,1,0:T(2,128)S(1)} copy-done((s32[1,1,2,2]{3,2,1,0:T(2,128)S(1)}, s32[1,1,2,2]{3,2,1,0:T(2,128)}, u32[]{:S(2)}) %copy-start.2) | copy-done | bytes 40
  25.9 0.6 prepare.1
  26.5 0.5 collective-permute-done.4.xfo
  26.9 1.7 %softmax.1 = (bf16[2,160,256]{2,1,0:T(8,128)(2,1)S(1)}, bf16[2,160,512]{2,1,0:T(8,128)(2,1)S(1)}, bf16[2,160,512]{2,1,0:T(8,128)(2,1)S(1)}, bf16[2,160,256]{2,1,...) custom-call(bf16[160,256]{1,0:T(8,128)(2,1)S(1)} %get-tuple-element., ...), custom_call_target="tpu_custom_call" | custom-call | flops 2000000000 | bytes 2097152 | tf_op jit(solution)/shard_map/softmax/pallas_call | solution.py:192
  28.6 3.6 %collective-permute-start.5 = (bf16[2,160,256]{2,1,0:T(8,128)(2,1)S(1)}, bf16[2,160,256]{2,1,0:T(8,128)(2,1)S(1)}, u32[]{:S(2)}, u32[]{:S(2)}) collective-permute-start(bf16[2,160,256]{2,1,0:T(8,128)(2,1)S(1)} %get-tuple-element.51), channel_id=1, source_target_pairs={{1,2},{2,1},{3,4},{4,3},{5,6},{6,5},{7,8},{8,7},{9,10},{10,9},{11,... | collective-permute-start | bytes 491528 | tf_op jit(solution)/shard_map/ppermute | solution.py:219
  32.2 0.6 keys.1
  32.8 2.5 %all-gather.1 = bf16[12,160,256]{2,1,0:T(8,128)(2,1)S(1)} all-gather(bf16[6,160,256]{2,1,0:T(8,128)(2,1)S(1)} %get-tuple-element.49), channel_id=3, replica_groups={{0,1},{2,3},{4,5},{6,7},{8,9},{10,11},{12,13},{14,15},{16,17},{18,19},{..., dimensions={0}, use_global_device_ids=true | all-gather | bytes 1474560 | tf_op jit(solution)/shard_map/all_gather | solution.py:221
  35.3 1.9 %collective-permute-start.6 = (bf16[2,160,256]{2,1,0:T(8,128)(2,1)S(1)}, bf16[2,160,256]{2,1,0:T(8,128)(2,1)S(1)}, u32[]{:S(2)}, u32[]{:S(2)}) collective-permute-start(bf16[2,160,256]{2,1,0:T(8,128)(2,1)S(1)} %get-tuple-element.55), channel_id=1, source_target_pairs={{0,16},{1,17},{2,18},{3,19},{4,20},{5,21},{6,22},{7,23},{8,24},{9,... | collective-permute-start | bytes 491528 | tf_op jit(solution)/shard_map/ppermute | solution.py:219
  37.2 0.1 dynamic-slice_convert_fusion
  37.3 0.0 collective-permute-done.5
  37.3 0.1 fusion.4
  37.4 3.9 %collective-permute-start.9 = (bf16[2,160,256]{2,1,0:T(8,128)(2,1)S(1)}, bf16[2,160,256]{2,1,0:T(8,128)(2,1)S(1)}, u32[]{:S(2)}, u32[]{:S(2)}) collective-permute-start(bf16[2,160,256]{2,1,0:T(8,128)(2,1)S(1)} %fusion.4), channel_id=1, source_target_pairs={{16,32},{17,33},{18,34},{19,35},{20,36},{21,37},{22,38},{23,39},{2... | collective-permute-start | bytes 491528 | tf_op jit(solution)/shard_map/ppermute | solution.py:219
  41.3 1.9 %collective-permute-start.8 = (bf16[2,160,256]{2,1,0:T(8,128)(2,1)S(1)}, bf16[2,160,256]{2,1,0:T(8,128)(2,1)S(1)}, u32[]{:S(2)}, u32[]{:S(2)}) collective-permute-start(bf16[2,160,256]{2,1,0:T(8,128)(2,1)S(1)} %fusion.1), channel_id=1, source_target_pairs={{0,16},{1,17},{2,18},{3,19},{4,20},{5,21},{6,22},{7,23},{8,24},{9,... | collective-permute-start | bytes 491528 | tf_op jit(solution)/shard_map/ppermute | solution.py:219
  43.3 0.0 collective-permute-done.6
  43.3 3.2 %collective-permute-start.7 = (bf16[2,160,256]{2,1,0:T(8,128)(2,1)S(1)}, bf16[2,160,256]{2,1,0:T(8,128)(2,1)S(1)}, u32[]{:S(2)}, u32[]{:S(2)}) collective-permute-start(bf16[2,160,256]{2,1,0:T(8,128)(2,1)S(1)} %add_convert_fusion), channel_id=1, source_target_pairs={{1,2},{2,1},{3,4},{4,3},{5,6},{6,5},{7,8},{8,7},{9,10},{10,9},{11,... | collective-permute-start | bytes 491528 | tf_op jit(solution)/shard_map/ppermute | solution.py:219
  46.6 1.2 %queries.1 = (bf16[160,256]{1,0:T(8,128)(2,1)}, bf16[160,256]{1,0:T(8,128)(2,1)}) custom-call(bf16[1280,256]{1,0:T(8,128)(2,1)S(1)} %get-tuple-element.38.ks, bf16[1280,256]{1,0:T(8,128)(2,1)S(1)} %get-tuple-element.39.vs, bf16[256,256]{1,0:T(8,128)(2,1)S(1)} %get-tuple-element.40.kc, bf16[256,256]{1,0:T(8,128)(2,1)S(1)} %get-tuple-element.41.vc, ...), custom_call_target="tpu_custom_call" | custom-call | flops 1000000000 | bytes 2097152 | tf_op jit(solution)/shard_map/queries/pallas_call | solution.py:192
  47.8 3.1 %collective-permute-done.9 = bf16[2,160,256]{2,1,0:T(8,128)(2,1)S(1)} collective-permute-done((bf16[2,160,256]{2,1,0:T(8,128)(2,1)S(1)}, bf16[2,160,256]{2,1,0:T(8,128)(2,1)S(1)}, u32[]{:S(2)}, u32[]{:S(2)}) %collective-permute-start.9) | collective-permute-done | bytes 163872 | tf_op jit(solution)/shard_map/ppermute | solution.py:219
  50.9 0.0 collective-permute-done.8
  50.9 6.7 %collective-permute-done.7 = bf16[2,160,256]{2,1,0:T(8,128)(2,1)S(1)} collective-permute-done((bf16[2,160,256]{2,1,0:T(8,128)(2,1)S(1)}, bf16[2,160,256]{2,1,0:T(8,128)(2,1)S(1)}, u32[]{:S(2)}, u32[]{:S(2)}) %collective-permute-start.7) | collective-permute-done | bytes 163872 | tf_op jit(solution)/shard_map/ppermute | solution.py:219
  57.6 0.1 fusion.9
  57.7 0.7 %fusion.10 = (bf16[1,160,256]{2,1,0:T(8,128)(2,1)}, bf16[1,160,256]{2,1,0:T(8,128)(2,1)}) fusion(bf16[2,160,256]{2,1,0:T(8,128)(2,1)S(1)} %fusion.9), kind=kLoop, calls=%fused_computation.17 | loop fusion | bytes 327680 | tf_op jit(solution)/shard_map/slice | solution.py:264
  (2 shorter events, 0.1 us)
Async XLA Ops:
  0.6 21.8 %copy-start.3 = (bf16[1,2,80,256]{3,2,1,0:T(8,128)(2,1)S(1)}, bf16[1,2,80,256]{3,2,1,0:T(8,128)(2,1)}, u32[]{:S(2)}) copy-start(bf16[1,2,80,256]{3,2,1,0:T(8,128)(2,1)} %param.7) | copy-start | bytes 245764
  0.6 21.8 %copy-start.4 = (bf16[1,2,80,256]{3,2,1,0:T(8,128)(2,1)S(1)}, bf16[1,2,80,256]{3,2,1,0:T(8,128)(2,1)}, u32[]{:S(2)}) copy-start(bf16[1,2,80,256]{3,2,1,0:T(8,128)(2,1)} %param.6) | copy-start | bytes 245764
  1.6 9.3 %collective-permute-start = (bf16[2,160,256]{2,1,0:T(8,128)(2,1)S(1)}, bf16[2,160,256]{2,1,0:T(8,128)(2,1)S(1)}, u32[]{:S(2)}, u32[]{:S(2)}) collective-permute-start(bf16[2,160,256]{2,1,0:T(8,128)(2,1)S(1)} %pad_maximum_fusion.1.x), channel_id=1, source_target_pairs={{1,2},{2,1},{3,4},{4,3},{5,6},{6,5},{7,8},{8,7},{9,10},{10,9},{11,... | collective-permute-start | bytes 491528 | tf_op jit(solution)/shard_map/ppermute | solution.py:219
  4.4 13.4 %collective-permute-start.2 = (bf16[2,160,256]{2,1,0:T(8,128)(2,1)S(1)}, bf16[2,160,256]{2,1,0:T(8,128)(2,1)S(1)}, u32[]{:S(2)}, u32[]{:S(2)}) collective-permute-start(bf16[2,160,256]{2,1,0:T(8,128)(2,1)S(1)} %pad_maximum_fusion.1.x), channel_id=1, source_target_pairs={{16,32},{17,33},{18,34},{19,35},{20,36},{21,37},{22,38},{23,39},{2... | collective-permute-start | bytes 491528 | tf_op jit(solution)/shard_map/ppermute | solution.py:219
  7.7 14.7 %collective-permute-start.3 = (bf16[2,160,256]{2,1,0:T(8,128)(2,1)S(1)}, bf16[2,160,256]{2,1,0:T(8,128)(2,1)S(1)}, u32[]{:S(2)}, u32[]{:S(2)}) collective-permute-start(bf16[2,160,256]{2,1,0:T(8,128)(2,1)S(1)} %pad_maximum_fusion.1.x), channel_id=1, source_target_pairs={{0,16},{1,17},{2,18},{3,19},{4,20},{5,21},{6,22},{7,23},{8,24},{9,... | collective-permute-start | bytes 491528 | tf_op jit(solution)/shard_map/ppermute | solution.py:219
  10.9 14.3 %collective-permute-start.1 = (bf16[2,160,256]{2,1,0:T(8,128)(2,1)S(1)}, bf16[2,160,256]{2,1,0:T(8,128)(2,1)S(1)}, u32[]{:S(2)}, u32[]{:S(2)}) collective-permute-start(bf16[2,160,256]{2,1,0:T(8,128)(2,1)S(1)} %collective-permute-done.xo), channel_id=1, source_target_pairs={{0,16},{1,17},{2,18},{3,19},{4,20},{5,21},{6,22},{7,23},{8,24},{9,... | collective-permute-start | bytes 491528 | tf_op jit(solution)/shard_map/ppermute | solution.py:219
  17.8 9.1 %collective-permute-start.4 = (bf16[2,160,256]{2,1,0:T(8,128)(2,1)S(1)}, bf16[2,160,256]{2,1,0:T(8,128)(2,1)S(1)}, u32[]{:S(2)}, u32[]{:S(2)}) collective-permute-start(bf16[2,160,256]{2,1,0:T(8,128)(2,1)S(1)} %collective-permute-done.2.xf), channel_id=1, source_target_pairs={{1,2},{2,1},{3,4},{4,3},{5,6},{6,5},{7,8},{8,7},{9,10},{10,9},{11,... | collective-permute-start | bytes 491528 | tf_op jit(solution)/shard_map/ppermute | solution.py:219
  22.5 2.7 %copy-start = (bf16[1,2,80,256]{3,2,1,0:T(8,128)(2,1)S(1)}, bf16[1,2,80,256]{3,2,1,0:T(8,128)(2,1)}, u32[]{:S(2)}) copy-start(bf16[1,2,80,256]{3,2,1,0:T(8,128)(2,1)} %param.5) | copy-start | bytes 245764
  22.5 2.7 %copy-start.1 = (bf16[1,2,80,256]{3,2,1,0:T(8,128)(2,1)S(1)}, bf16[1,2,80,256]{3,2,1,0:T(8,128)(2,1)}, u32[]{:S(2)}) copy-start(bf16[1,2,80,256]{3,2,1,0:T(8,128)(2,1)} %param.8) | copy-start | bytes 245764
  25.2 0.7 %copy-start.2 = (s32[1,1,2,2]{3,2,1,0:T(2,128)S(1)}, s32[1,1,2,2]{3,2,1,0:T(2,128)}, u32[]{:S(2)}) copy-start(s32[1,1,2,2]{3,2,1,0:T(2,128)} %reach) | copy-start | bytes 52
  28.6 8.7 %collective-permute-start.5 = (bf16[2,160,256]{2,1,0:T(8,128)(2,1)S(1)}, bf16[2,160,256]{2,1,0:T(8,128)(2,1)S(1)}, u32[]{:S(2)}, u32[]{:S(2)}) collective-permute-start(bf16[2,160,256]{2,1,0:T(8,128)(2,1)S(1)} %get-tuple-element.51), channel_id=1, source_target_pairs={{1,2},{2,1},{3,4},{4,3},{5,6},{6,5},{7,8},{8,7},{9,10},{10,9},{11,... | collective-permute-start | bytes 491528 | tf_op jit(solution)/shard_map/ppermute | solution.py:219
  35.3 8.0 %collective-permute-start.6 = (bf16[2,160,256]{2,1,0:T(8,128)(2,1)S(1)}, bf16[2,160,256]{2,1,0:T(8,128)(2,1)S(1)}, u32[]{:S(2)}, u32[]{:S(2)}) collective-permute-start(bf16[2,160,256]{2,1,0:T(8,128)(2,1)S(1)} %get-tuple-element.55), channel_id=1, source_target_pairs={{0,16},{1,17},{2,18},{3,19},{4,20},{5,21},{6,22},{7,23},{8,24},{9,... | collective-permute-start | bytes 491528 | tf_op jit(solution)/shard_map/ppermute | solution.py:219
  37.4 13.5 %collective-permute-start.9 = (bf16[2,160,256]{2,1,0:T(8,128)(2,1)S(1)}, bf16[2,160,256]{2,1,0:T(8,128)(2,1)S(1)}, u32[]{:S(2)}, u32[]{:S(2)}) collective-permute-start(bf16[2,160,256]{2,1,0:T(8,128)(2,1)S(1)} %fusion.4), channel_id=1, source_target_pairs={{16,32},{17,33},{18,34},{19,35},{20,36},{21,37},{22,38},{23,39},{2... | collective-permute-start | bytes 491528 | tf_op jit(solution)/shard_map/ppermute | solution.py:219
  41.3 9.6 %collective-permute-start.8 = (bf16[2,160,256]{2,1,0:T(8,128)(2,1)S(1)}, bf16[2,160,256]{2,1,0:T(8,128)(2,1)S(1)}, u32[]{:S(2)}, u32[]{:S(2)}) collective-permute-start(bf16[2,160,256]{2,1,0:T(8,128)(2,1)S(1)} %fusion.1), channel_id=1, source_target_pairs={{0,16},{1,17},{2,18},{3,19},{4,20},{5,21},{6,22},{7,23},{8,24},{9,... | collective-permute-start | bytes 491528 | tf_op jit(solution)/shard_map/ppermute | solution.py:219
  43.3 14.3 %collective-permute-start.7 = (bf16[2,160,256]{2,1,0:T(8,128)(2,1)S(1)}, bf16[2,160,256]{2,1,0:T(8,128)(2,1)S(1)}, u32[]{:S(2)}, u32[]{:S(2)}) collective-permute-start(bf16[2,160,256]{2,1,0:T(8,128)(2,1)S(1)} %add_convert_fusion), channel_id=1, source_target_pairs={{1,2},{2,1},{3,4},{4,3},{5,6},{6,5},{7,8},{8,7},{9,10},{10,9},{11,... | collective-permute-start | bytes 491528 | tf_op jit(solution)/shard_map/ppermute | solution.py:219
